TPU v7x, 32 devices: a whole 2x2x4 slice. The times are simulated.
32 devices in a mesh: blk: 16 (over z, x, core), rep: 2 (over y).
Axes of the slice: x: 2, y: 2, z: 4, core: 2. Of those that a mesh axis runs over, the one named last changes fastest.
Arguments:
- block_inputs: bfloat16 [5120, 4096], P(('blk', 'rep')), may hold values from -120 to 120
- out_cotangent: bfloat16 [5120, 4096], P(('blk', 'rep')), may hold values from -6 to 6
- dnormed_in: float32 [5120, 4096], P(('blk', 'rep')), may hold values from -6 to 6
- carried_sums: float32 [3, 1792, 4096], P(None, ('blk', 'rep')), may hold values from -128 to 128
- norm_gain: float32 [4096], replicated, may hold values from 0.1 to 1.9
- w_gate: bfloat16 [896, 4096], P('blk'), may hold values from -0.09375 to 0.09375
- w_up: bfloat16 [896, 4096], P('blk'), may hold values from -0.09375 to 0.09375
- w_down: bfloat16 [896, 4096], P('blk'), may hold values from -0.1875 to 0.1875
Outputs:
- input_grad: bfloat16 [5120, 4096], P(('blk', 'rep'))
- grad_gate: bfloat16 [896, 4096], P('blk')
- grad_up: bfloat16 [896, 4096], P('blk')
- grad_down: bfloat16 [896, 4096], P('blk')
All inputs are finite; a program needn't handle non-finite values.
Results may differ from a plain program's by a relative error of at most 0.0038.
Values may be sent and summed in bfloat16 or wider, within the bound.
A program may use at most 64 MiB of HBM per device.

v0:
```python
import math

import jax
import jax.numpy as jnp
from jax import lax
from jax.sharding import PartitionSpec as P

CYCLE_STEPS = 6


epsilon = 1e-05


def passed_along(value, axis, steps):
    count = lax.axis_size(axis)
    pairs = [(source, (source + steps) % count) for source in range(count)]
    return lax.ppermute(value, axis, pairs)


def local_terms(normed, grad_in, gate_rows, up_rows, down_rows):
    gate = jnp.einsum("td,fd->tf", normed, gate_rows, preferred_element_type=jnp.float32)
    upper = jnp.einsum("td,fd->tf", normed, up_rows, preferred_element_type=jnp.float32)
    sigma = jax.nn.sigmoid(gate)
    act = gate * sigma
    hidden = (act * upper).astype(jnp.bfloat16)
    dhidden = jnp.einsum("td,fd->tf", grad_in, down_rows, preferred_element_type=jnp.float32)
    dgate = (dhidden * upper * sigma * (1.0 + gate * (1.0 - sigma))).astype(jnp.bfloat16)
    dup = (dhidden * act).astype(jnp.bfloat16)
    dnormed = jnp.einsum("tf,fd->td", dgate, gate_rows, preferred_element_type=jnp.float32)
    dnormed = dnormed + jnp.einsum("tf,fd->td", dup, up_rows, preferred_element_type=jnp.float32)
    terms = (
        jnp.einsum("tf,td->fd", dgate, normed, preferred_element_type=jnp.float32),
        jnp.einsum("tf,td->fd", dup, normed, preferred_element_type=jnp.float32),
        jnp.einsum("tf,td->fd", hidden, grad_in, preferred_element_type=jnp.float32),
    )
    return (terms, dnormed)


def shards(block_inputs, out_cotangent, dnormed_in, carried_sums, norm_gain, w_gate, w_up, w_down):
    steps = CYCLE_STEPS
    scale = 1.0 / math.sqrt(lax.axis_size("blk") * block_inputs.shape[0] * lax.axis_size("rep"))
    values = block_inputs.astype(jnp.float32)
    rstd = lax.rsqrt(jnp.mean(values * values, axis=-1, keepdims=True) + epsilon)
    normed = (values * rstd * norm_gain).astype(jnp.bfloat16)
    weights = passed_along((w_gate, w_up, w_down), "blk", -steps)
    terms, part = local_terms(normed, out_cotangent, weights[0], weights[1], weights[2])
    dnormed = dnormed_in + part
    fresh = (carried_sums[0] + terms[0], carried_sums[1] + terms[1], carried_sums[2] + terms[2])
    sums = fresh

    def advance(index, state):
        weights_now, sums_now, dnormed_now = state
        weights_now = passed_along((weights_now[0], weights_now[1], weights_now[2]), "blk", 1)
        step_terms, step_part = local_terms(
            normed, out_cotangent, weights_now[0], weights_now[1], weights_now[2]
        )
        dnormed_now = dnormed_now + step_part
        moved = passed_along((sums_now[0], sums_now[1], sums_now[2]), "blk", 1)
        sums_now = (moved[0] + step_terms[0], moved[1] + step_terms[1], moved[2] + step_terms[2])
        return (weights_now, sums_now, dnormed_now)

    weights, sums, dnormed = lax.fori_loop(1, steps, advance, (weights, sums, dnormed))
    home = passed_along((sums[0], sums[1], sums[2]), "blk", 1)
    halves = (
        lax.psum_scatter(home[0], "rep", scatter_dimension=1, tiled=True),
        lax.psum_scatter(home[1], "rep", scatter_dimension=1, tiled=True),
        lax.psum_scatter(home[2], "rep", scatter_dimension=1, tiled=True),
    )
    rounded = tuple(((piece * scale).astype(jnp.bfloat16) for piece in halves))
    finals = (
        lax.all_gather(rounded[0], "rep", axis=1, tiled=True),
        lax.all_gather(rounded[1], "rep", axis=1, tiled=True),
        lax.all_gather(rounded[2], "rep", axis=1, tiled=True),
    )
    scaled = norm_gain * dnormed
    dx = rstd * scaled - values * rstd**3 * jnp.mean(values * scaled, axis=-1, keepdims=True)
    input_grad = (out_cotangent.astype(jnp.float32) + dx).astype(jnp.bfloat16)
    return (input_grad, finals[0], finals[1], finals[2])


def solution(mesh):
    placed = (
        P(("blk", "rep"), None),
        P(("blk", "rep"), None),
        P(("blk", "rep"), None),
        P(None, ("blk", "rep"), None),
        P(),
        P("blk", None),
        P("blk", None),
        P("blk", None),
    )
    return jax.shard_map(
        shards,
        mesh=mesh,
        in_specs=placed,
        out_specs=(P(("blk", "rep"), None), P("blk", None), P("blk", None), P("blk", None)),
        check_vma=False,
    )
```

profile of v0, /device:TPU:0, one launch (start us, length us, event | category | flops | bytes accessed | tf_op | source)
XLA Modules:
  0.0 437.4 jit_solution(4228410990701043142)
XLA Ops:
  7.2 5.0 %collective-permute-start.6 = (bf16[56,4096]{1,0:T(8,128)(2,1)}, bf16[56,4096]{1,0:T(8,128)(2,1)S(1)}, u32[]{:S(2)}, u32[]{:S(2)}) collective-permute-start(bf16[56,4096]{1,0:T(8,128)(2,1)} %param.15), channel_id=1, source_target_pairs={{0,20},{2,22},{4,24},{6,26},{8,28},{10,30},{12,0},{14,2},{16,4},{1... | collective-permute-start | bytes 1376264 | tf_op jit(solution)/shard_map/ppermute | solution.py:17
  12.6 3.5 collective-permute-start.8
  16.2 1.7 fusion.5
  18.9 1.8 fusion.7
  20.8 2.7 collective-permute-done.6
  24.1 9.3 %collective-permute-done.7 = bf16[56,4096]{1,0:T(8,128)(2,1)} collective-permute-done((bf16[56,4096]{1,0:T(8,128)(2,1)}, bf16[56,4096]{1,0:T(8,128)(2,1)}, u32[]{:S(2)}, u32[]{:S(2)}) %collective-permute-start.7) | collective-permute-done | bytes 458784 | tf_op jit(solution)/shard_map/ppermute | solution.py:17
  36.2 5.8 %collective-permute-done.8 = bf16[56,4096]{1,0:T(8,128)(2,1)S(1)} collective-permute-done((bf16[56,4096]{1,0:T(8,128)(2,1)}, bf16[56,4096]{1,0:T(8,128)(2,1)S(1)}, u32[]{:S(2)}, u32[]{:S(2)}) %collective-permute-start.8) | collective-permute-done | bytes 458784 | tf_op jit(solution)/shard_map/ppermute | solution.py:17
  46.7 2.0 fusion.4
  48.8 290.6 %while.22 = (s32[]{:T(128)}, bf16[56,4096]{1,0:T(8,128)(2,1)S(1)}, bf16[56,4096]{1,0:T(8,128)(2,1)}, bf16[56,4096]{1,0:T(8,128)(2,1)S(1)}, f32[56,4096]{1,0:T(8,...) while((s32[]{:T(128)}, bf16[56,4096]{1,0:T(8,128)(2,1)S(1)}, ...), condition=%wide.region_2.0_spmd, body=%wide.region_1.0_spmd.sunk | while | flops 589371648 | bytes 74051080 | solution.py:62
  50.3 31.0 %collective-permute-start = (bf16[56,4096]{1,0:T(8,128)(2,1)}, bf16[56,4096]{1,0:T(8,128)(2,1)S(1)}, u32[]{:S(2)}, u32[]{:S(2)}) collective-permute-start(bf16[56,4096]{1,0:T(8,128)(2,1)} %copy-done.6), channel_id=1, source_target_pairs={{0,2},{2,4},{4,6},{6,8},{8,10},{10,12},{12,14},{14,16},{16,18},{18... | collective-permute-start | bytes 1376264 | tf_op jit(solution)/shard_map/while/body/eval_jaxpr/ppermute | solution.py:17
  82.9 7.1 %collective-permute-done.1 = bf16[56,4096]{1,0:T(8,128)(2,1)S(1)} collective-permute-done((bf16[56,4096]{1,0:T(8,128)(2,1)}, bf16[56,4096]{1,0:T(8,128)(2,1)S(1)}, u32[]{:S(2)}, u32[]{:S(2)}) %collective-permute-start.1) | collective-permute-done | bytes 458784 | tf_op jit(solution)/shard_map/while/body/eval_jaxpr/ppermute | solution.py:17
  90.8 4.1 collective-permute-done
  96.9 3.1 collective-permute-done.2
  100.0 1.8 copy.31
  101.8 1.7 multiply_convert_fusion.14
  105.0 14.6 %collective-permute-done.4 = f32[56,4096]{1,0:T(8,128)} collective-permute-done((f32[56,4096]{1,0:T(8,128)}, f32[56,4096]{1,0:T(8,128)}, u32[]{:S(2)}, u32[]{:S(2)}) %collective-permute-start.4) | collective-permute-done | bytes 917536 | tf_op jit(solution)/shard_map/while/body/eval_jaxpr/ppermute | solution.py:17
  119.6 2.5 convolution_add_fusion.12
  122.1 2.5 convolution_add_fusion.13
  124.7 4.7 %collective-permute-done.3 = f32[56,4096]{1,0:T(8,128)S(1)} collective-permute-done((f32[56,4096]{1,0:T(8,128)}, f32[56,4096]{1,0:T(8,128)S(1)}, u32[]{:S(2)}, u32[]{:S(2)}) %collective-permute-start.3) | collective-permute-done | bytes 917536 | tf_op jit(solution)/shard_map/while/body/eval_jaxpr/ppermute | solution.py:17
  133.3 8.9 %collective-permute-done.1 = bf16[56,4096]{1,0:T(8,128)(2,1)S(1)} collective-permute-done((bf16[56,4096]{1,0:T(8,128)(2,1)}, bf16[56,4096]{1,0:T(8,128)(2,1)S(1)}, u32[]{:S(2)}, u32[]{:S(2)}) %collective-permute-start.1) | collective-permute-done | bytes 458784 | tf_op jit(solution)/shard_map/while/body/eval_jaxpr/ppermute | solution.py:17
  143.0 4.1 collective-permute-done
  149.0 3.1 collective-permute-done.2
  152.2 1.8 copy.31
  154.0 1.7 multiply_convert_fusion.14
  157.2 14.6 %collective-permute-done.4 = f32[56,4096]{1,0:T(8,128)} collective-permute-done((f32[56,4096]{1,0:T(8,128)}, f32[56,4096]{1,0:T(8,128)}, u32[]{:S(2)}, u32[]{:S(2)}) %collective-permute-start.4) | collective-permute-done | bytes 917536 | tf_op jit(solution)/shard_map/while/body/eval_jaxpr/ppermute | solution.py:17
  171.8 2.5 convolution_add_fusion.12
  174.3 2.5 convolution_add_fusion.13
  176.9 4.7 %collective-permute-done.3 = f32[56,4096]{1,0:T(8,128)S(1)} collective-permute-done((f32[56,4096]{1,0:T(8,128)}, f32[56,4096]{1,0:T(8,128)S(1)}, u32[]{:S(2)}, u32[]{:S(2)}) %collective-permute-start.3) | collective-permute-done | bytes 917536 | tf_op jit(solution)/shard_map/while/body/eval_jaxpr/ppermute | solution.py:17
  184.4 10.0 %collective-permute-done.1 = bf16[56,4096]{1,0:T(8,128)(2,1)S(1)} collective-permute-done((bf16[56,4096]{1,0:T(8,128)(2,1)}, bf16[56,4096]{1,0:T(8,128)(2,1)S(1)}, u32[]{:S(2)}, u32[]{:S(2)}) %collective-permute-start.1) | collective-permute-done | bytes 458784 | tf_op jit(solution)/shard_map/while/body/eval_jaxpr/ppermute | solution.py:17
  195.2 4.1 collective-permute-done
  201.2 3.1 collective-permute-done.2
  204.3 1.8 copy.31
  206.2 1.7 multiply_convert_fusion.14
  209.4 14.6 %collective-permute-done.4 = f32[56,4096]{1,0:T(8,128)} collective-permute-done((f32[56,4096]{1,0:T(8,128)}, f32[56,4096]{1,0:T(8,128)}, u32[]{:S(2)}, u32[]{:S(2)}) %collective-permute-start.4) | collective-permute-done | bytes 917536 | tf_op jit(solution)/shard_map/while/body/eval_jaxpr/ppermute | solution.py:17
  224.0 2.5 convolution_add_fusion.12
  226.5 2.5 convolution_add_fusion.13
  229.0 4.7 %collective-permute-done.3 = f32[56,4096]{1,0:T(8,128)S(1)} collective-permute-done((f32[56,4096]{1,0:T(8,128)}, f32[56,4096]{1,0:T(8,128)S(1)}, u32[]{:S(2)}, u32[]{:S(2)}) %collective-permute-start.3) | collective-permute-done | bytes 917536 | tf_op jit(solution)/shard_map/while/body/eval_jaxpr/ppermute | solution.py:17
  236.6 10.0 %collective-permute-done.1 = bf16[56,4096]{1,0:T(8,128)(2,1)S(1)} collective-permute-done((bf16[56,4096]{1,0:T(8,128)(2,1)}, bf16[56,4096]{1,0:T(8,128)(2,1)S(1)}, u32[]{:S(2)}, u32[]{:S(2)}) %collective-permute-start.1) | collective-permute-done | bytes 458784 | tf_op jit(solution)/shard_map/while/body/eval_jaxpr/ppermute | solution.py:17
  247.4 4.1 collective-permute-done
  253.4 3.1 collective-permute-done.2
  256.5 1.8 copy.31
  258.3 1.7 multiply_convert_fusion.14
  261.5 14.6 %collective-permute-done.4 = f32[56,4096]{1,0:T(8,128)} collective-permute-done((f32[56,4096]{1,0:T(8,128)}, f32[56,4096]{1,0:T(8,128)}, u32[]{:S(2)}, u32[]{:S(2)}) %collective-permute-start.4) | collective-permute-done | bytes 917536 | tf_op jit(solution)/shard_map/while/body/eval_jaxpr/ppermute | solution.py:17
  276.2 2.5 convolution_add_fusion.12
  278.7 2.5 convolution_add_fusion.13
  281.2 4.7 %collective-permute-done.3 = f32[56,4096]{1,0:T(8,128)S(1)} collective-permute-done((f32[56,4096]{1,0:T(8,128)}, f32[56,4096]{1,0:T(8,128)S(1)}, u32[]{:S(2)}, u32[]{:S(2)}) %collective-permute-start.3) | collective-permute-done | bytes 917536 | tf_op jit(solution)/shard_map/while/body/eval_jaxpr/ppermute | solution.py:17
  288.8 10.0 %collective-permute-done.1 = bf16[56,4096]{1,0:T(8,128)(2,1)S(1)} collective-permute-done((bf16[56,4096]{1,0:T(8,128)(2,1)}, bf16[56,4096]{1,0:T(8,128)(2,1)S(1)}, u32[]{:S(2)}, u32[]{:S(2)}) %collective-permute-start.1) | collective-permute-done | bytes 458784 | tf_op jit(solution)/shard_map/while/body/eval_jaxpr/ppermute | solution.py:17
  299.5 4.1 collective-permute-done
  305.6 3.1 collective-permute-done.2
  308.7 1.8 copy.31
  310.5 1.7 multiply_convert_fusion.14
  313.7 14.6 %collective-permute-done.4 = f32[56,4096]{1,0:T(8,128)} collective-permute-done((f32[56,4096]{1,0:T(8,128)}, f32[56,4096]{1,0:T(8,128)}, u32[]{:S(2)}, u32[]{:S(2)}) %collective-permute-start.4) | collective-permute-done | bytes 917536 | tf_op jit(solution)/shard_map/while/body/eval_jaxpr/ppermute | solution.py:17
  328.4 2.5 convolution_add_fusion.12
  330.9 2.5 convolution_add_fusion.13
  333.4 4.7 %collective-permute-done.3 = f32[56,4096]{1,0:T(8,128)S(1)} collective-permute-done((f32[56,4096]{1,0:T(8,128)}, f32[56,4096]{1,0:T(8,128)S(1)}, u32[]{:S(2)}, u32[]{:S(2)}) %collective-permute-start.3) | collective-permute-done | bytes 917536 | tf_op jit(solution)/shard_map/while/body/eval_jaxpr/ppermute | solution.py:17
  339.4 15.7 %collective-permute-done.9 = f32[56,4096]{1,0:T(8,128)S(1)} collective-permute-done((f32[56,4096]{1,0:T(8,128)}, f32[56,4096]{1,0:T(8,128)S(1)}, u32[]{:S(2)}, u32[]{:S(2)}) %collective-permute-start.9) | collective-permute-done | bytes 917536 | tf_op jit(solution)/shard_map/ppermute | solution.py:17
  356.2 15.7 %collective-permute-done.10 = f32[56,4096]{1,0:T(8,128)S(1)} collective-permute-done((f32[56,4096]{1,0:T(8,128)}, f32[56,4096]{1,0:T(8,128)S(1)}, u32[]{:S(2)}, u32[]{:S(2)}) %collective-permute-start.10) | collective-permute-done | bytes 917536 | tf_op jit(solution)/shard_map/ppermute | solution.py:17
  373.0 2.2 fusion.12
  375.8 13.0 %collective-permute-done.11 = f32[56,4096]{1,0:T(8,128)S(1)} collective-permute-done((f32[56,4096]{1,0:T(8,128)}, f32[56,4096]{1,0:T(8,128)S(1)}, u32[]{:S(2)}, u32[]{:S(2)}) %collective-permute-start.11) | collective-permute-done | bytes 917536 | tf_op jit(solution)/shard_map/ppermute | solution.py:17
  389.7 3.8 fusion.11
  394.6 7.8 %all_gather.9 = bf16[56,4096]{1,0:T(8,128)(2,1)S(1)} all-gather(bf16[56,2048]{1,0:T(8,128)(2,1)S(1)} %multiply_convert_fusion.6), channel_id=1, replica_groups=mesh['blk'=16,'rep'=2] {'rep'}, dimensions={1}, use_global_device_ids=true | all-gather | bytes 688128 | tf_op jit(solution)/shard_map/all_gather | solution.py:71
  403.5 12.1 %all_gather.10 = bf16[56,4096]{1,0:T(8,128)(2,1)S(1)} all-gather(bf16[56,2048]{1,0:T(8,128)(2,1)S(1)} %multiply_convert_fusion.5), channel_id=1, replica_groups=mesh['blk'=16,'rep'=2] {'rep'}, dimensions={1}, use_global_device_ids=true | all-gather | bytes 688128 | tf_op jit(solution)/shard_map/all_gather | solution.py:72
  415.6 3.9 reduce-scatter.8.cloned.1.call-done
  420.6 8.0 %all_gather.11 = bf16[56,4096]{1,0:T(8,128)(2,1)S(1)} all-gather(bf16[56,2048]{1,0:T(8,128)(2,1)S(1)} %multiply_convert_fusion.4), channel_id=1, replica_groups=mesh['blk'=16,'rep'=2] {'rep'}, dimensions={1}, use_global_device_ids=true | all-gather | bytes 688128 | tf_op jit(solution)/shard_map/all_gather | solution.py:73
  (174 shorter events, 56.5 us)
Async XLA Ops:
  7.2 386.4 %reduce-scatter.4.cloned.1.call-start = ((), (), s32[]{:S(2)}) async-start(), calls=%async_computation.3 | async-start | bytes 1376256 | tf_op jit(solution)/shard_map/reduce_scatter | solution.py:65
  7.2 16.3 %collective-permute-start.6 = (bf16[56,4096]{1,0:T(8,128)(2,1)}, bf16[56,4096]{1,0:T(8,128)(2,1)S(1)}, u32[]{:S(2)}, u32[]{:S(2)}) collective-permute-start(bf16[56,4096]{1,0:T(8,128)(2,1)} %param.15), channel_id=1, source_target_pairs={{0,20},{2,22},{4,24},{6,26},{8,28},{10,30},{12,0},{14,2},{16,4},{1... | collective-permute-start | bytes 1376264 | tf_op jit(solution)/shard_map/ppermute | solution.py:17
  12.2 21.1 %collective-permute-start.7 = (bf16[56,4096]{1,0:T(8,128)(2,1)}, bf16[56,4096]{1,0:T(8,128)(2,1)}, u32[]{:S(2)}, u32[]{:S(2)}) collective-permute-start(bf16[56,4096]{1,0:T(8,128)(2,1)} %param.16), channel_id=1, source_target_pairs={{0,20},{2,22},{4,24},{6,26},{8,28},{10,30},{12,0},{14,2},{16,4},{1... | collective-permute-start | bytes 1376264 | tf_op jit(solution)/shard_map/ppermute | solution.py:17
  12.6 29.4 %collective-permute-start.8 = (bf16[56,4096]{1,0:T(8,128)(2,1)}, bf16[56,4096]{1,0:T(8,128)(2,1)S(1)}, u32[]{:S(2)}, u32[]{:S(2)}) collective-permute-start(bf16[56,4096]{1,0:T(8,128)(2,1)} %param.17), channel_id=1, source_target_pairs={{0,20},{2,22},{4,24},{6,26},{8,28},{10,30},{12,0},{14,2},{16,4},{1... | collective-permute-start | bytes 1376264 | tf_op jit(solution)/shard_map/ppermute | solution.py:17
  18.9 16.0 %copy-start = (bf16[160,4096]{1,0:T(8,128)(2,1)S(1)}, bf16[160,4096]{1,0:T(8,128)(2,1)}, u32[]{:S(2)}) copy-start(bf16[160,4096]{1,0:T(8,128)(2,1)} %param.11) | copy-start | bytes 3932164
  20.8 14.2 %copy-start.4 = (f32[3,56,4096]{2,1,0:T(8,128)S(1)}, f32[3,56,4096]{2,1,0:T(8,128)}, u32[]{:S(2)}) copy-start(f32[3,56,4096]{2,1,0:T(8,128)} %param.13) | copy-start | bytes 8257540
  43.9 2.8 copy-start.5
  48.8 324.2 %copy-start.13 = (f32[4096]{0:T(1024)S(1)}, f32[4096]{0:T(1024)}, u32[]{:S(2)}) copy-start(f32[4096]{0:T(1024)} %param.14) | copy-start | bytes 49156
  49.5 40.5 %collective-permute-start.1 = (bf16[56,4096]{1,0:T(8,128)(2,1)}, bf16[56,4096]{1,0:T(8,128)(2,1)S(1)}, u32[]{:S(2)}, u32[]{:S(2)}) collective-permute-start(bf16[56,4096]{1,0:T(8,128)(2,1)} %get-tuple-element.167), channel_id=1, source_target_pairs={{0,2},{2,4},{4,6},{6,8},{8,10},{10,12},{12,14},{14,16},{16,18},{18... | collective-permute-start | bytes 1376264 | tf_op jit(solution)/shard_map/while/body/eval_jaxpr/ppermute | solution.py:17
  50.3 44.7 %collective-permute-start = (bf16[56,4096]{1,0:T(8,128)(2,1)}, bf16[56,4096]{1,0:T(8,128)(2,1)S(1)}, u32[]{:S(2)}, u32[]{:S(2)}) collective-permute-start(bf16[56,4096]{1,0:T(8,128)(2,1)} %copy-done.6), channel_id=1, source_target_pairs={{0,2},{2,4},{4,6},{6,8},{8,10},{10,12},{12,14},{14,16},{16,18},{18... | collective-permute-start | bytes 1376264 | tf_op jit(solution)/shard_map/while/body/eval_jaxpr/ppermute | solution.py:17
  81.3 18.7 %collective-permute-start.2 = (bf16[56,4096]{1,0:T(8,128)(2,1)}, bf16[56,4096]{1,0:T(8,128)(2,1)}, u32[]{:S(2)}, u32[]{:S(2)}) collective-permute-start(bf16[56,4096]{1,0:T(8,128)(2,1)} %copy-done.11), channel_id=1, source_target_pairs={{0,2},{2,4},{4,6},{6,8},{8,10},{10,12},{12,14},{14,16},{16,18},{18... | collective-permute-start | bytes 1376264 | tf_op jit(solution)/shard_map/while/body/eval_jaxpr/ppermute | solution.py:17
  82.0 40.1 %collective-permute-start.5 = (f32[56,4096]{1,0:T(8,128)}, f32[56,4096]{1,0:T(8,128)}, u32[]{:S(2)}, u32[]{:S(2)}) collective-permute-start(f32[56,4096]{1,0:T(8,128)} %get-tuple-element.171), channel_id=1, source_target_pairs={{0,2},{2,4},{4,6},{6,8},{8,10},{10,12},{12,14},{14,16},{16,18},{18... | collective-permute-start | bytes 2752520 | tf_op jit(solution)/shard_map/while/body/eval_jaxpr/ppermute | solution.py:17
  82.2 37.5 %collective-permute-start.4 = (f32[56,4096]{1,0:T(8,128)}, f32[56,4096]{1,0:T(8,128)}, u32[]{:S(2)}, u32[]{:S(2)}) collective-permute-start(f32[56,4096]{1,0:T(8,128)} %get-tuple-element.170), channel_id=1, source_target_pairs={{0,2},{2,4},{4,6},{6,8},{8,10},{10,12},{12,14},{14,16},{16,18},{18... | collective-permute-start | bytes 2752520 | tf_op jit(solution)/shard_map/while/body/eval_jaxpr/ppermute | solution.py:17
  90.0 39.3 %collective-permute-start.3 = (f32[56,4096]{1,0:T(8,128)}, f32[56,4096]{1,0:T(8,128)S(1)}, u32[]{:S(2)}, u32[]{:S(2)}) collective-permute-start(f32[56,4096]{1,0:T(8,128)} %get-tuple-element.169), channel_id=1, source_target_pairs={{0,2},{2,4},{4,6},{6,8},{8,10},{10,12},{12,14},{14,16},{16,18},{18... | collective-permute-start | bytes 2752520 | tf_op jit(solution)/shard_map/while/body/eval_jaxpr/ppermute | solution.py:17
  101.8 2.3 copy-start.1
  105.0 19.7 %copy-start.2 = (f32[160,4096]{1,0:T(8,128)}, f32[160,4096]{1,0:T(8,128)S(1)}, u32[]{:S(2)}) copy-start(f32[160,4096]{1,0:T(8,128)S(1)} %fusion.89) | copy-start | bytes 7864324 | tf_op jit(solution)/shard_map/while
  122.1 8.5 %copy-start.7 = (bf16[56,4096]{1,0:T(8,128)(2,1)S(1)}, bf16[56,4096]{1,0:T(8,128)(2,1)}, u32[]{:S(2)}) copy-start(bf16[56,4096]{1,0:T(8,128)(2,1)} %copy.29) | copy-start | bytes 1376260 | tf_op jit(solution)/shard_map/while
  122.1 8.5 %copy-start.12 = (bf16[56,4096]{1,0:T(8,128)(2,1)S(1)}, bf16[56,4096]{1,0:T(8,128)(2,1)}, u32[]{:S(2)}) copy-start(bf16[56,4096]{1,0:T(8,128)(2,1)} %copy.31) | copy-start | bytes 1376260 | tf_op jit(solution)/shard_map/while
  131.4 10.8 %collective-permute-start.1 = (bf16[56,4096]{1,0:T(8,128)(2,1)}, bf16[56,4096]{1,0:T(8,128)(2,1)S(1)}, u32[]{:S(2)}, u32[]{:S(2)}) collective-permute-start(bf16[56,4096]{1,0:T(8,128)(2,1)} %get-tuple-element.167), channel_id=1, source_target_pairs={{0,2},{2,4},{4,6},{6,8},{8,10},{10,12},{12,14},{14,16},{16,18},{18... | collective-permute-start | bytes 1376264 | tf_op jit(solution)/shard_map/while/body/eval_jaxpr/ppermute | solution.py:17
  132.2 15.0 %collective-permute-start = (bf16[56,4096]{1,0:T(8,128)(2,1)}, bf16[56,4096]{1,0:T(8,128)(2,1)S(1)}, u32[]{:S(2)}, u32[]{:S(2)}) collective-permute-start(bf16[56,4096]{1,0:T(8,128)(2,1)} %copy-done.6), channel_id=1, source_target_pairs={{0,2},{2,4},{4,6},{6,8},{8,10},{10,12},{12,14},{14,16},{16,18},{18... | collective-permute-start | bytes 1376264 | tf_op jit(solution)/shard_map/while/body/eval_jaxpr/ppermute | solution.py:17
  132.2 20.0 %collective-permute-start.2 = (bf16[56,4096]{1,0:T(8,128)(2,1)}, bf16[56,4096]{1,0:T(8,128)(2,1)}, u32[]{:S(2)}, u32[]{:S(2)}) collective-permute-start(bf16[56,4096]{1,0:T(8,128)(2,1)} %copy-done.11), channel_id=1, source_target_pairs={{0,2},{2,4},{4,6},{6,8},{8,10},{10,12},{12,14},{14,16},{16,18},{18... | collective-permute-start | bytes 1376264 | tf_op jit(solution)/shard_map/while/body/eval_jaxpr/ppermute | solution.py:17
  132.2 42.1 %collective-permute-start.5 = (f32[56,4096]{1,0:T(8,128)}, f32[56,4096]{1,0:T(8,128)}, u32[]{:S(2)}, u32[]{:S(2)}) collective-permute-start(f32[56,4096]{1,0:T(8,128)} %get-tuple-element.171), channel_id=1, source_target_pairs={{0,2},{2,4},{4,6},{6,8},{8,10},{10,12},{12,14},{14,16},{16,18},{18... | collective-permute-start | bytes 2752520 | tf_op jit(solution)/shard_map/while/body/eval_jaxpr/ppermute | solution.py:17
  132.5 39.3 %collective-permute-start.4 = (f32[56,4096]{1,0:T(8,128)}, f32[56,4096]{1,0:T(8,128)}, u32[]{:S(2)}, u32[]{:S(2)}) collective-permute-start(f32[56,4096]{1,0:T(8,128)} %get-tuple-element.170), channel_id=1, source_target_pairs={{0,2},{2,4},{4,6},{6,8},{8,10},{10,12},{12,14},{14,16},{16,18},{18... | collective-permute-start | bytes 2752520 | tf_op jit(solution)/shard_map/while/body/eval_jaxpr/ppermute | solution.py:17
  142.2 39.3 %collective-permute-start.3 = (f32[56,4096]{1,0:T(8,128)}, f32[56,4096]{1,0:T(8,128)S(1)}, u32[]{:S(2)}, u32[]{:S(2)}) collective-permute-start(f32[56,4096]{1,0:T(8,128)} %get-tuple-element.169), channel_id=1, source_target_pairs={{0,2},{2,4},{4,6},{6,8},{8,10},{10,12},{12,14},{14,16},{16,18},{18... | collective-permute-start | bytes 2752520 | tf_op jit(solution)/shard_map/while/body/eval_jaxpr/ppermute | solution.py:17
  154.0 2.3 copy-start.1
  157.2 19.7 %copy-start.2 = (f32[160,4096]{1,0:T(8,128)}, f32[160,4096]{1,0:T(8,128)S(1)}, u32[]{:S(2)}) copy-start(f32[160,4096]{1,0:T(8,128)S(1)} %fusion.89) | copy-start | bytes 7864324 | tf_op jit(solution)/shard_map/while
  174.3 8.5 %copy-start.7 = (bf16[56,4096]{1,0:T(8,128)(2,1)S(1)}, bf16[56,4096]{1,0:T(8,128)(2,1)}, u32[]{:S(2)}) copy-start(bf16[56,4096]{1,0:T(8,128)(2,1)} %copy.29) | copy-start | bytes 1376260 | tf_op jit(solution)/shard_map/while
  174.3 8.5 %copy-start.12 = (bf16[56,4096]{1,0:T(8,128)(2,1)S(1)}, bf16[56,4096]{1,0:T(8,128)(2,1)}, u32[]{:S(2)}) copy-start(bf16[56,4096]{1,0:T(8,128)(2,1)} %copy.31) | copy-start | bytes 1376260 | tf_op jit(solution)/shard_map/while
  183.6 10.8 %collective-permute-start.1 = (bf16[56,4096]{1,0:T(8,128)(2,1)}, bf16[56,4096]{1,0:T(8,128)(2,1)S(1)}, u32[]{:S(2)}, u32[]{:S(2)}) collective-permute-start(bf16[56,4096]{1,0:T(8,128)(2,1)} %get-tuple-element.167), channel_id=1, source_target_pairs={{0,2},{2,4},{4,6},{6,8},{8,10},{10,12},{12,14},{14,16},{16,18},{18... | collective-permute-start | bytes 1376264 | tf_op jit(solution)/shard_map/while/body/eval_jaxpr/ppermute | solution.py:17
  184.4 15.0 %collective-permute-start = (bf16[56,4096]{1,0:T(8,128)(2,1)}, bf16[56,4096]{1,0:T(8,128)(2,1)S(1)}, u32[]{:S(2)}, u32[]{:S(2)}) collective-permute-start(bf16[56,4096]{1,0:T(8,128)(2,1)} %copy-done.6), channel_id=1, source_target_pairs={{0,2},{2,4},{4,6},{6,8},{8,10},{10,12},{12,14},{14,16},{16,18},{18... | collective-permute-start | bytes 1376264 | tf_op jit(solution)/shard_map/while/body/eval_jaxpr/ppermute | solution.py:17
  184.4 20.0 %collective-permute-start.2 = (bf16[56,4096]{1,0:T(8,128)(2,1)}, bf16[56,4096]{1,0:T(8,128)(2,1)}, u32[]{:S(2)}, u32[]{:S(2)}) collective-permute-start(bf16[56,4096]{1,0:T(8,128)(2,1)} %copy-done.11), channel_id=1, source_target_pairs={{0,2},{2,4},{4,6},{6,8},{8,10},{10,12},{12,14},{14,16},{16,18},{18... | collective-permute-start | bytes 1376264 | tf_op jit(solution)/shard_map/while/body/eval_jaxpr/ppermute | solution.py:17
  184.4 42.1 %collective-permute-start.5 = (f32[56,4096]{1,0:T(8,128)}, f32[56,4096]{1,0:T(8,128)}, u32[]{:S(2)}, u32[]{:S(2)}) collective-permute-start(f32[56,4096]{1,0:T(8,128)} %get-tuple-element.171), channel_id=1, source_target_pairs={{0,2},{2,4},{4,6},{6,8},{8,10},{10,12},{12,14},{14,16},{16,18},{18... | collective-permute-start | bytes 2752520 | tf_op jit(solution)/shard_map/while/body/eval_jaxpr/ppermute | solution.py:17
  184.4 39.6 %collective-permute-start.4 = (f32[56,4096]{1,0:T(8,128)}, f32[56,4096]{1,0:T(8,128)}, u32[]{:S(2)}, u32[]{:S(2)}) collective-permute-start(f32[56,4096]{1,0:T(8,128)} %get-tuple-element.170), channel_id=1, source_target_pairs={{0,2},{2,4},{4,6},{6,8},{8,10},{10,12},{12,14},{14,16},{16,18},{18... | collective-permute-start | bytes 2752520 | tf_op jit(solution)/shard_map/while/body/eval_jaxpr/ppermute | solution.py:17
  194.4 39.3 %collective-permute-start.3 = (f32[56,4096]{1,0:T(8,128)}, f32[56,4096]{1,0:T(8,128)S(1)}, u32[]{:S(2)}, u32[]{:S(2)}) collective-permute-start(f32[56,4096]{1,0:T(8,128)} %get-tuple-element.169), channel_id=1, source_target_pairs={{0,2},{2,4},{4,6},{6,8},{8,10},{10,12},{12,14},{14,16},{16,18},{18... | collective-permute-start | bytes 2752520 | tf_op jit(solution)/shard_map/while/body/eval_jaxpr/ppermute | solution.py:17
  206.2 2.3 copy-start.1
  209.4 19.7 %copy-start.2 = (f32[160,4096]{1,0:T(8,128)}, f32[160,4096]{1,0:T(8,128)S(1)}, u32[]{:S(2)}) copy-start(f32[160,4096]{1,0:T(8,128)S(1)} %fusion.89) | copy-start | bytes 7864324 | tf_op jit(solution)/shard_map/while
  226.5 8.5 %copy-start.7 = (bf16[56,4096]{1,0:T(8,128)(2,1)S(1)}, bf16[56,4096]{1,0:T(8,128)(2,1)}, u32[]{:S(2)}) copy-start(bf16[56,4096]{1,0:T(8,128)(2,1)} %copy.29) | copy-start | bytes 1376260 | tf_op jit(solution)/shard_map/while
  226.5 8.5 %copy-start.12 = (bf16[56,4096]{1,0:T(8,128)(2,1)S(1)}, bf16[56,4096]{1,0:T(8,128)(2,1)}, u32[]{:S(2)}) copy-start(bf16[56,4096]{1,0:T(8,128)(2,1)} %copy.31) | copy-start | bytes 1376260 | tf_op jit(solution)/shard_map/while
  235.8 10.8 %collective-permute-start.1 = (bf16[56,4096]{1,0:T(8,128)(2,1)}, bf16[56,4096]{1,0:T(8,128)(2,1)S(1)}, u32[]{:S(2)}, u32[]{:S(2)}) collective-permute-start(bf16[56,4096]{1,0:T(8,128)(2,1)} %get-tuple-element.167), channel_id=1, source_target_pairs={{0,2},{2,4},{4,6},{6,8},{8,10},{10,12},{12,14},{14,16},{16,18},{18... | collective-permute-start | bytes 1376264 | tf_op jit(solution)/shard_map/while/body/eval_jaxpr/ppermute | solution.py:17
  236.5 15.0 %collective-permute-start = (bf16[56,4096]{1,0:T(8,128)(2,1)}, bf16[56,4096]{1,0:T(8,128)(2,1)S(1)}, u32[]{:S(2)}, u32[]{:S(2)}) collective-permute-start(bf16[56,4096]{1,0:T(8,128)(2,1)} %copy-done.6), channel_id=1, source_target_pairs={{0,2},{2,4},{4,6},{6,8},{8,10},{10,12},{12,14},{14,16},{16,18},{18... | collective-permute-start | bytes 1376264 | tf_op jit(solution)/shard_map/while/body/eval_jaxpr/ppermute | solution.py:17
  236.5 20.0 %collective-permute-start.2 = (bf16[56,4096]{1,0:T(8,128)(2,1)}, bf16[56,4096]{1,0:T(8,128)(2,1)}, u32[]{:S(2)}, u32[]{:S(2)}) collective-permute-start(bf16[56,4096]{1,0:T(8,128)(2,1)} %copy-done.11), channel_id=1, source_target_pairs={{0,2},{2,4},{4,6},{6,8},{8,10},{10,12},{12,14},{14,16},{16,18},{18... | collective-permute-start | bytes 1376264 | tf_op jit(solution)/shard_map/while/body/eval_jaxpr/ppermute | solution.py:17
  236.5 42.1 %collective-permute-start.5 = (f32[56,4096]{1,0:T(8,128)}, f32[56,4096]{1,0:T(8,128)}, u32[]{:S(2)}, u32[]{:S(2)}) collective-permute-start(f32[56,4096]{1,0:T(8,128)} %get-tuple-element.171), channel_id=1, source_target_pairs={{0,2},{2,4},{4,6},{6,8},{8,10},{10,12},{12,14},{14,16},{16,18},{18... | collective-permute-start | bytes 2752520 | tf_op jit(solution)/shard_map/while/body/eval_jaxpr/ppermute | solution.py:17
  236.5 39.6 %collective-permute-start.4 = (f32[56,4096]{1,0:T(8,128)}, f32[56,4096]{1,0:T(8,128)}, u32[]{:S(2)}, u32[]{:S(2)}) collective-permute-start(f32[56,4096]{1,0:T(8,128)} %get-tuple-element.170), channel_id=1, source_target_pairs={{0,2},{2,4},{4,6},{6,8},{8,10},{10,12},{12,14},{14,16},{16,18},{18... | collective-permute-start | bytes 2752520 | tf_op jit(solution)/shard_map/while/body/eval_jaxpr/ppermute | solution.py:17
  246.6 39.3 %collective-permute-start.3 = (f32[56,4096]{1,0:T(8,128)}, f32[56,4096]{1,0:T(8,128)S(1)}, u32[]{:S(2)}, u32[]{:S(2)}) collective-permute-start(f32[56,4096]{1,0:T(8,128)} %get-tuple-element.169), channel_id=1, source_target_pairs={{0,2},{2,4},{4,6},{6,8},{8,10},{10,12},{12,14},{14,16},{16,18},{18... | collective-permute-start | bytes 2752520 | tf_op jit(solution)/shard_map/while/body/eval_jaxpr/ppermute | solution.py:17
  258.3 2.3 copy-start.1
  261.5 19.7 %copy-start.2 = (f32[160,4096]{1,0:T(8,128)}, f32[160,4096]{1,0:T(8,128)S(1)}, u32[]{:S(2)}) copy-start(f32[160,4096]{1,0:T(8,128)S(1)} %fusion.89) | copy-start | bytes 7864324 | tf_op jit(solution)/shard_map/while
  278.7 8.5 %copy-start.7 = (bf16[56,4096]{1,0:T(8,128)(2,1)S(1)}, bf16[56,4096]{1,0:T(8,128)(2,1)}, u32[]{:S(2)}) copy-start(bf16[56,4096]{1,0:T(8,128)(2,1)} %copy.29) | copy-start | bytes 1376260 | tf_op jit(solution)/shard_map/while
  278.7 8.5 %copy-start.12 = (bf16[56,4096]{1,0:T(8,128)(2,1)S(1)}, bf16[56,4096]{1,0:T(8,128)(2,1)}, u32[]{:S(2)}) copy-start(bf16[56,4096]{1,0:T(8,128)(2,1)} %copy.31) | copy-start | bytes 1376260 | tf_op jit(solution)/shard_map/while
  287.9 10.8 %collective-permute-start.1 = (bf16[56,4096]{1,0:T(8,128)(2,1)}, bf16[56,4096]{1,0:T(8,128)(2,1)S(1)}, u32[]{:S(2)}, u32[]{:S(2)}) collective-permute-start(bf16[56,4096]{1,0:T(8,128)(2,1)} %get-tuple-element.167), channel_id=1, source_target_pairs={{0,2},{2,4},{4,6},{6,8},{8,10},{10,12},{12,14},{14,16},{16,18},{18... | collective-permute-start | bytes 1376264 | tf_op jit(solution)/shard_map/while/body/eval_jaxpr/ppermute | solution.py:17
  288.7 15.0 %collective-permute-start = (bf16[56,4096]{1,0:T(8,128)(2,1)}, bf16[56,4096]{1,0:T(8,128)(2,1)S(1)}, u32[]{:S(2)}, u32[]{:S(2)}) collective-permute-start(bf16[56,4096]{1,0:T(8,128)(2,1)} %copy-done.6), channel_id=1, source_target_pairs={{0,2},{2,4},{4,6},{6,8},{8,10},{10,12},{12,14},{14,16},{16,18},{18... | collective-permute-start | bytes 1376264 | tf_op jit(solution)/shard_map/while/body/eval_jaxpr/ppermute | solution.py:17
  288.7 20.0 %collective-permute-start.2 = (bf16[56,4096]{1,0:T(8,128)(2,1)}, bf16[56,4096]{1,0:T(8,128)(2,1)}, u32[]{:S(2)}, u32[]{:S(2)}) collective-permute-start(bf16[56,4096]{1,0:T(8,128)(2,1)} %copy-done.11), channel_id=1, source_target_pairs={{0,2},{2,4},{4,6},{6,8},{8,10},{10,12},{12,14},{14,16},{16,18},{18... | collective-permute-start | bytes 1376264 | tf_op jit(solution)/shard_map/while/body/eval_jaxpr/ppermute | solution.py:17
  288.7 42.1 %collective-permute-start.5 = (f32[56,4096]{1,0:T(8,128)}, f32[56,4096]{1,0:T(8,128)}, u32[]{:S(2)}, u32[]{:S(2)}) collective-permute-start(f32[56,4096]{1,0:T(8,128)} %get-tuple-element.171), channel_id=1, source_target_pairs={{0,2},{2,4},{4,6},{6,8},{8,10},{10,12},{12,14},{14,16},{16,18},{18... | collective-permute-start | bytes 2752520 | tf_op jit(solution)/shard_map/while/body/eval_jaxpr/ppermute | solution.py:17
  288.7 39.6 %collective-permute-start.4 = (f32[56,4096]{1,0:T(8,128)}, f32[56,4096]{1,0:T(8,128)}, u32[]{:S(2)}, u32[]{:S(2)}) collective-permute-start(f32[56,4096]{1,0:T(8,128)} %get-tuple-element.170), channel_id=1, source_target_pairs={{0,2},{2,4},{4,6},{6,8},{8,10},{10,12},{12,14},{14,16},{16,18},{18... | collective-permute-start | bytes 2752520 | tf_op jit(solution)/shard_map/while/body/eval_jaxpr/ppermute | solution.py:17
  298.8 39.3 %collective-permute-start.3 = (f32[56,4096]{1,0:T(8,128)}, f32[56,4096]{1,0:T(8,128)S(1)}, u32[]{:S(2)}, u32[]{:S(2)}) collective-permute-start(f32[56,4096]{1,0:T(8,128)} %get-tuple-element.169), channel_id=1, source_target_pairs={{0,2},{2,4},{4,6},{6,8},{8,10},{10,12},{12,14},{14,16},{16,18},{18... | collective-permute-start | bytes 2752520 | tf_op jit(solution)/shard_map/while/body/eval_jaxpr/ppermute | solution.py:17
  310.5 2.3 copy-start.1
  313.7 19.7 %copy-start.2 = (f32[160,4096]{1,0:T(8,128)}, f32[160,4096]{1,0:T(8,128)S(1)}, u32[]{:S(2)}) copy-start(f32[160,4096]{1,0:T(8,128)S(1)} %fusion.89) | copy-start | bytes 7864324 | tf_op jit(solution)/shard_map/while
  330.8 8.5 %copy-start.7 = (bf16[56,4096]{1,0:T(8,128)(2,1)S(1)}, bf16[56,4096]{1,0:T(8,128)(2,1)}, u32[]{:S(2)}) copy-start(bf16[56,4096]{1,0:T(8,128)(2,1)} %copy.29) | copy-start | bytes 1376260 | tf_op jit(solution)/shard_map/while
  330.8 8.5 %copy-start.12 = (bf16[56,4096]{1,0:T(8,128)(2,1)S(1)}, bf16[56,4096]{1,0:T(8,128)(2,1)}, u32[]{:S(2)}) copy-start(bf16[56,4096]{1,0:T(8,128)(2,1)} %copy.31) | copy-start | bytes 1376260 | tf_op jit(solution)/shard_map/while
  339.4 33.7 %copy-start.3 = (bf16[160,4096]{1,0:T(8,128)(2,1)S(1)}, bf16[160,4096]{1,0:T(8,128)(2,1)}, u32[]{:S(2)}) copy-start(bf16[160,4096]{1,0:T(8,128)(2,1)} %param.10) | copy-start | bytes 3932164
  339.4 15.8 %collective-permute-start.9 = (f32[56,4096]{1,0:T(8,128)}, f32[56,4096]{1,0:T(8,128)S(1)}, u32[]{:S(2)}, u32[]{:S(2)}) collective-permute-start(f32[56,4096]{1,0:T(8,128)} %get-tuple-element.60), channel_id=1, source_target_pairs={{0,2},{2,4},{4,6},{6,8},{8,10},{10,12},{12,14},{14,16},{16,18},{18... | collective-permute-start | bytes 2752520 | tf_op jit(solution)/shard_map/ppermute | solution.py:17
  356.1 46.4 %reduce-scatter.6.cloned.1.call-start = ((), (), s32[]{:S(2)}) async-start(), calls=%async_computation.4 | async-start | bytes 1376256 | tf_op jit(solution)/shard_map/reduce_scatter | solution.py:66
  356.1 15.8 %collective-permute-start.10 = (f32[56,4096]{1,0:T(8,128)}, f32[56,4096]{1,0:T(8,128)S(1)}, u32[]{:S(2)}, u32[]{:S(2)}) collective-permute-start(f32[56,4096]{1,0:T(8,128)} %get-tuple-element.61), channel_id=1, source_target_pairs={{0,2},{2,4},{4,6},{6,8},{8,10},{10,12},{12,14},{14,16},{16,18},{18... | collective-permute-start | bytes 2752520 | tf_op jit(solution)/shard_map/ppermute | solution.py:17
  372.9 46.6 %reduce-scatter.8.cloned.1.call-start = ((), (), s32[]{:S(2)}) async-start(), calls=%async_computation.5 | async-start | bytes 1376256 | tf_op jit(solution)/shard_map/reduce_scatter | solution.py:67
  372.9 15.8 %collective-permute-start.11 = (f32[56,4096]{1,0:T(8,128)}, f32[56,4096]{1,0:T(8,128)S(1)}, u32[]{:S(2)}, u32[]{:S(2)}) collective-permute-start(f32[56,4096]{1,0:T(8,128)} %get-tuple-element.62), channel_id=1, source_target_pairs={{0,2},{2,4},{4,6},{6,8},{8,10},{10,12},{12,14},{14,16},{16,18},{18... | collective-permute-start | bytes 2752520 | tf_op jit(solution)/shard_map/ppermute | solution.py:17
  (14 other events, 11.1 us)
Sparse Core Ops, SparseCore 0:
  356.2 16.1 reduce-scatter.3
  374.7 21.3 reduce-scatter.5
  398.3 21.1 reduce-scatter.7
where the time goes:
time: 439 us; the launch traced here: 437 us
  waiting for transfers between devices  245 us (56%)
  matrix products  63.1 us (14%)
  starting transfers between devices  43.2 us (10%)
  local copies, waits for them, and re-layouts  30.2 us (7%)
  blocking collectives  27.9 us (6%)
  between operations  13.9 us (3%)
  other arithmetic  13.8 us (3%)
    ppermute x36, waiting for transfers between devices, passed_along(): return lax.ppermute(value, axis, pairs)  241 us
    ppermute x36, starting transfers between devices, passed_along(): return lax.ppermute(value, axis, pairs)  43.1 us
    while x75, local copies, waits for them, and re-layouts  24.5 us
    dot_general x6, matrix products, local_terms(): jnp.einsum('tf,td->fd', hidden, grad_in, preferred_element_type=jnp.float32)  14 us
    dot_general x6, matrix products, local_terms(): jnp.einsum('tf,td->fd', dup, normed, preferred_element_type=jnp.float32)  13.8 us
    all_gather x1, blocking collectives, shards(): lax.all_gather(rounded[1], 'rep', axis=1, tiled=True)  12.1 us
    dot_general x6, matrix products, local_terms(): jnp.einsum('td,fd->tf', grad_in, down_rows, preferred_element_type=jnp.fl...  9.23 us
  transfers between devices with their start and end apart: 39, of which 32 were waited for; matrix products, arithmetic and copies ran while one was open for 18% of the time, Pallas kernels for 0%

commit v1 on v0

v1 whole, which is shorter than its diff:
```python
import math

import jax
import jax.numpy as jnp
from jax import lax
from jax.sharding import PartitionSpec as P

CYCLE_STEPS = 6
CORES = 2
HOPS = CYCLE_STEPS // CORES

CHAIN = jnp.bfloat16
REP = jnp.bfloat16
SWAP = jnp.float32

epsilon = 1e-05


def moved(value, steps):
    count = lax.axis_size("blk")
    return lax.ppermute(value, "blk", [(i, (i + steps) % count) for i in range(count)])


def swapped_core(value):
    count = lax.axis_size("blk")
    return lax.ppermute(value, "blk", [(i, i ^ 1) for i in range(count)])


def swapped_rep(value):
    count = lax.axis_size("rep")
    return lax.ppermute(value, "rep", [(i, (i + 1) % count) for i in range(count)])


def swapped_rep_upper(value):
    reps = lax.axis_size("rep")
    pairs = [
        (i * reps + r, i * reps + (r + 1) % reps)
        for i in range(1, lax.axis_size("blk"), CORES)
        for r in range(reps)
    ]
    return lax.ppermute(value, ("blk", "rep"), pairs)


def group_terms(normed, grad_in, first, second, units):
    gu_rows = jnp.concatenate([first[: 2 * units], second[: 2 * units]], axis=0)
    down_rows = jnp.concatenate([first[2 * units :], second[2 * units :]], axis=0)
    gu = jnp.einsum("td,fd->tf", normed, gu_rows, preferred_element_type=jnp.float32)
    dhidden = jnp.einsum("td,fd->tf", grad_in, down_rows, preferred_element_type=jnp.float32)
    gu = gu.reshape(gu.shape[0], 2, 2, units)
    gate, upper = gu[:, :, 0], gu[:, :, 1]
    dhidden = dhidden.reshape(gate.shape)
    sigma = jax.nn.sigmoid(gate)
    act = gate * sigma
    hidden = (act * upper).astype(jnp.bfloat16).reshape(gate.shape[0], 2 * units)
    dgate = (dhidden * upper * sigma * (1.0 + gate * (1.0 - sigma))).astype(jnp.bfloat16)
    dup = (dhidden * act).astype(jnp.bfloat16)
    dgu = jnp.stack([dgate, dup], axis=2).reshape(gate.shape[0], 4 * units)
    dnormed = jnp.einsum("tf,fd->td", dgu, gu_rows, preferred_element_type=jnp.float32)
    t_gu = jnp.einsum("tf,td->fd", dgu, normed, preferred_element_type=jnp.float32)
    t_down = jnp.einsum("tf,td->fd", hidden, grad_in, preferred_element_type=jnp.float32)
    own = jnp.concatenate([t_gu[: 2 * units], t_down[:units]], axis=0)
    other = jnp.concatenate([t_gu[2 * units :], t_down[units:]], axis=0)
    return own, other, dnormed


def shards(block_inputs, out_cotangent, dnormed_in, carried_sums, norm_gain, w_gate, w_up, w_down):
    reps = lax.axis_size("rep")
    scale = 1.0 / math.sqrt(lax.axis_size("blk") * block_inputs.shape[0] * reps)
    core = lax.rem(lax.axis_index("blk"), CORES)
    rep = lax.axis_index("rep")
    units, width = w_gate.shape
    half = width // 2

    def mine(v):
        return lax.dynamic_slice_in_dim(v, rep * half, half, axis=v.ndim - 1)

    def theirs(v):
        return lax.dynamic_slice_in_dim(v, (1 - rep) * half, half, axis=v.ndim - 1)

    def joined(a, b):
        return jnp.where(rep == 0, jnp.concatenate([a, b], -1), jnp.concatenate([b, a], -1))

    def summed(v):
        return mine(v) + swapped_rep(theirs(v).astype(REP)).astype(jnp.float32)

    own_weights = jnp.concatenate([w_gate, w_up, w_down], axis=0)
    piece = mine(own_weights)
    fulls = []
    for _ in range(HOPS):
        piece = moved(piece, -CORES)
        fulls.append(joined(piece, swapped_rep(piece)))

    carried = carried_sums.reshape(3 * units, width)
    held = None
    if CHAIN != jnp.float32:
        held = mine(carried) + swapped_rep(theirs(carried))
        held = moved(held, CYCLE_STEPS)

    values = block_inputs.astype(jnp.float32)
    rstd = lax.rsqrt(jnp.mean(values * values, axis=-1, keepdims=True) + epsilon)
    normed = (values * rstd * norm_gain).astype(jnp.bfloat16)

    dnormed = dnormed_in
    reduced = []
    for j in range(HOPS):
        if j < HOPS - 1:
            other = swapped_core(fulls[j])
        else:
            other = swapped_core(jnp.where(core == 0, fulls[j], own_weights))
        own_term, other_term, part = group_terms(normed, out_cotangent, fulls[j], other, units)
        dnormed = dnormed + part
        received = swapped_core(other_term.astype(SWAP)).astype(jnp.float32)
        if j < HOPS - 1:
            reduced.append(own_term + received)
        else:
            last = own_term + jnp.where(core == 0, received, 0.0)
            if held is None:
                last = last + carried
            reduced.append(last)
            near = mine(received) + swapped_rep_upper(theirs(received).astype(REP)).astype(
                jnp.float32
            )
            near = jnp.where(core == 0, 0.0, near)

    sums = summed(reduced[HOPS - 1])
    for j in range(HOPS - 2, -1, -1):
        sums = moved(sums.astype(CHAIN), CORES).astype(jnp.float32) + summed(reduced[j])
    sums = moved(sums.astype(CHAIN), CORES).astype(jnp.float32) + near
    if held is not None:
        sums = sums + held
    rounded = (sums * scale).astype(jnp.bfloat16)
    finals = joined(rounded, swapped_rep(rounded))

    scaled = norm_gain * dnormed
    dx = rstd * scaled - values * rstd**3 * jnp.mean(values * scaled, axis=-1, keepdims=True)
    input_grad = (out_cotangent.astype(jnp.float32) + dx).astype(jnp.bfloat16)
    return (input_grad, finals[:units], finals[units : 2 * units], finals[2 * units :])


def solution(mesh):
    placed = (
        P(("blk", "rep"), None),
        P(("blk", "rep"), None),
        P(("blk", "rep"), None),
        P(None, ("blk", "rep"), None),
        P(),
        P("blk", None),
        P("blk", None),
        P("blk", None),
    )
    return jax.shard_map(
        shards,
        mesh=mesh,
        in_specs=placed,
        out_specs=(P(("blk", "rep"), None), P("blk", None), P("blk", None), P("blk", None)),
        check_vma=False,
    )
```

time: 439 us -> 244 us (0.56)
  waiting for transfers between devices: 245 us -> 141 us
  matrix products: 63.1 us -> 16.1 us
  blocking collectives: 27.9 us -> 0 us
  between operations: 13.9 us -> 1.48 us
  starting transfers between devices: 43.2 us -> 30.9 us
  other arithmetic: 13.8 us -> 19.3 us
    ppermute x36 -> x22, waiting for transfers between devices: 241 us -> 141 us  [the longest x8 86.1 us: swapped_rep(): lax.ppermute(value, 'rep', [(i, (i + 1) % count) for i in range(count)])]
    dot_general x48 -> x15, matrix products: 63.1 us -> 16.1 us  [the longest x3 4.21 us: group_terms(): jnp.einsum('tf,td->fd', dgu, normed, preferred_element_type=jnp.float32)]
    all_gather x3 -> x0, blocking collectives: 27.9 us -> none  [the longest x1 12.1 us: shards(): lax.all_gather(rounded[1], 'rep', axis=1, tiled=True)]
    while x75 -> x0, local copies, waits for them, and re-layouts: 24.5 us -> none
    slice x0 -> x22, local copies, waits for them, and re-layouts: none -> 17 us  [the longest x6 6.06 us: group_terms(): own = jnp.concatenate([t_gu[:2 * units], t_down[:units]], axis=0)]
    ppermute x36 -> x22, starting transfers between devices: 43.1 us -> 30.9 us  [the longest x7 16.8 us: moved(): lax.ppermute(value, 'blk', [(i, (i + steps) % count) for i in range(count)])]
    select_n x0 -> x4, other arithmetic: none -> 6.09 us  [the longest x3 4.28 us: joined(): jnp.where(rep == 0, jnp.concatenate([a, b], -1), jnp.concatenate([b, a],...]
    dot_general x0 -> x3, local copies, waits for them, and re-layouts: none -> 4.88 us  [group_terms(): jnp.einsum('td,fd->tf', grad_in, down_rows, preferred_element_type=jnp.fl...]
  transfers between devices with their start and end apart: 39 -> 22, of which waited for: 32 -> 14; matrix products, arithmetic and copies ran while one was open for 18% -> 23% of each run, Pallas kernels for 0% -> 0%
where the time goes in v1:
time: 244 us; the launch traced here: 243 us
  waiting for transfers between devices  141 us (58%)
  local copies, waits for them, and re-layouts  33.8 us (14%)
  starting transfers between devices  30.9 us (13%)
  other arithmetic  19.3 us (8%)
  matrix products  16.1 us (7%)
    ppermute x8, waiting for transfers between devices, swapped_rep(): lax.ppermute(value, 'rep', [(i, (i + 1) % count) for i in range(count)])  86.1 us
    ppermute x7, waiting for transfers between devices, moved(): lax.ppermute(value, 'blk', [(i, (i + steps) % count) for i in range(count)])  52.8 us
    ppermute x7, starting transfers between devices, moved(): lax.ppermute(value, 'blk', [(i, (i + steps) % count) for i in range(count)])  16.8 us
    ppermute x8, starting transfers between devices, swapped_rep(): lax.ppermute(value, 'rep', [(i, (i + 1) % count) for i in range(count)])  11.5 us
    unnamed x80, local copies, waits for them, and re-layouts  8.78 us
    slice x6, local copies, waits for them, and re-layouts, group_terms(): own = jnp.concatenate([t_gu[:2 * units], t_down[:units]], axis=0)  6.06 us
    slice x6, local copies, waits for them, and re-layouts, group_terms(): gu_rows = jnp.concatenate([first[:2 * units], second[:2 * units]], axis=0)  4.95 us
    dot_general x3, local copies, waits for them, and re-layouts, group_terms(): jnp.einsum('td,fd->tf', grad_in, down_rows, preferred_element_type=jnp.fl...  4.88 us
  transfers between devices with their start and end apart: 22, of which 14 were waited for; matrix products, arithmetic and copies ran while one was open for 23% of the time, Pallas kernels for 0%

profile of v1, /device:TPU:0, one launch (start us, length us, event | category | flops | bytes accessed | tf_op | source)
XLA Modules:
  0.0 242.8 jit_solution(864389969639509959)
XLA Ops:
  0.6 1.1 constant_dynamic-update-slice_fusion.2
  1.8 1.1 constant_dynamic-update-slice_fusion.1
  2.9 6.0 %collective-permute-start = (bf16[168,2048]{1,0:T(8,128)(2,1)S(1)}, bf16[168,2048]{1,0:T(8,128)(2,1)}, u32[]{:S(2)}, u32[]{:S(2)}) collective-permute-start(bf16[168,2048]{1,0:T(8,128)(2,1)S(1)} %constant_dynamic-slice_fusion.1), channel_id=1, source_target_pairs={{0,28},{2,30},{4,0},{6,2},{8,4},{10,6},{12,8},{14,10},{16,12},{18,... | collective-permute-start | bytes 2064392 | tf_op jit(solution)/shard_map/ppermute | solution.py:21
  9.0 14.7 %collective-permute-done = bf16[168,2048]{1,0:T(8,128)(2,1)} collective-permute-done((bf16[168,2048]{1,0:T(8,128)(2,1)S(1)}, bf16[168,2048]{1,0:T(8,128)(2,1)}, u32[]{:S(2)}, u32[]{:S(2)}) %collective-permute-start) | collective-permute-done | bytes 688160 | tf_op jit(solution)/shard_map/ppermute | solution.py:21
  23.7 5.3 %collective-permute-start.3 = (bf16[168,2048]{1,0:T(8,128)(2,1)}, bf16[168,2048]{1,0:T(8,128)(2,1)S(1)}, u32[]{:S(2)}, u32[]{:S(2)}) collective-permute-start(bf16[168,2048]{1,0:T(8,128)(2,1)} %collective-permute-done), channel_id=1, source_target_pairs={{0,28},{2,30},{4,0},{6,2},{8,4},{10,6},{12,8},{14,10},{16,12},{18,... | collective-permute-start | bytes 2064392 | tf_op jit(solution)/shard_map/ppermute | solution.py:21
  29.0 2.6 %constant_dynamic-slice_fusion = f32[168,2048]{1,0:T(8,128)} fusion(f32[168,4096]{1,0:T(8,128)} %bitcast.178, s32[]{:T(128)S(6)} %select_n.63), kind=kLoop, calls=%fused_computation.122 | loop fusion | bytes 2752516 | tf_op jit(solution)/shard_map/dynamic_slice | solution.py:78
  31.5 1.5 collective-permute-start.19
  33.9 9.2 %collective-permute-done.3 = bf16[168,2048]{1,0:T(8,128)(2,1)S(1)} collective-permute-done((bf16[168,2048]{1,0:T(8,128)(2,1)}, bf16[168,2048]{1,0:T(8,128)(2,1)S(1)}, u32[]{:S(2)}, u32[]{:S(2)}) %collective-permute-start.3) | collective-permute-done | bytes 688160 | tf_op jit(solution)/shard_map/ppermute | solution.py:21
  43.1 5.1 %collective-permute-start.6 = (bf16[168,2048]{1,0:T(8,128)(2,1)S(1)}, bf16[168,2048]{1,0:T(8,128)(2,1)S(1)}, u32[]{:S(2)}, u32[]{:S(2)}) collective-permute-start(bf16[168,2048]{1,0:T(8,128)(2,1)S(1)} %collective-permute-done.3), channel_id=1, source_target_pairs={{0,28},{2,30},{4,0},{6,2},{8,4},{10,6},{12,8},{14,10},{16,12},{18,... | collective-permute-start | bytes 2064392 | tf_op jit(solution)/shard_map/ppermute | solution.py:21
  48.7 1.5 collective-permute-start.4
  50.2 29.5 %collective-permute-done.1 = bf16[168,2048]{1,0:T(8,128)(2,1)} collective-permute-done((bf16[168,2048]{1,0:T(8,128)(2,1)}, bf16[168,2048]{1,0:T(8,128)(2,1)}, u32[]{:S(2)}, u32[]{:S(2)}) %collective-permute-start.1) | collective-permute-done | bytes 688160 | tf_op jit(solution)/shard_map/ppermute | solution.py:31
  79.7 2.2 maximum_select_fusion
  82.0 1.6 collective-permute-start.7
  83.6 2.7 %dynamic-slice_add_fusion = f32[168,2048]{1,0:T(8,128)} fusion(f32[168,2048]{1,0:T(8,128)} %collective-permute-done.19, f32[168,4096]{1,0:T(8,128)S(1)} %bitcast.179, s32[]{:T(128)S(6)} %select_n.56), kind=kLoop, calls=%fused_computation.30 | loop fusion | flops 344064 | bytes 4128772 | tf_op jit(solution)/shard_map/add | solution.py:96
  86.5 7.9 %collective-permute-done.4 = bf16[168,2048]{1,0:T(8,128)(2,1)S(1)} collective-permute-done((bf16[168,2048]{1,0:T(8,128)(2,1)S(1)}, bf16[168,2048]{1,0:T(8,128)(2,1)S(1)}, u32[]{:S(2)}, u32[]{:S(2)}) %collective-permute-start.4) | collective-permute-done | bytes 688160 | tf_op jit(solution)/shard_map/ppermute | solution.py:31
  94.4 1.6 maximum_select_fusion.1
  96.0 2.2 slice.140
  98.2 1.8 slice.138
  100.0 6.8 %collective-permute-done.7 = bf16[168,2048]{1,0:T(8,128)(2,1)S(1)} collective-permute-done((bf16[168,2048]{1,0:T(8,128)(2,1)S(1)}, bf16[168,2048]{1,0:T(8,128)(2,1)S(1)}, u32[]{:S(2)}, u32[]{:S(2)}) %collective-permute-start.7) | collective-permute-done | bytes 688160 | tf_op jit(solution)/shard_map/ppermute | solution.py:31
  106.8 1.8 broadcast_select_fusion
  108.7 0.9 slice.144
  109.7 0.7 fusion.15
  111.3 1.7 fusion.94
  113.0 1.2 convolution_bitcast_fusion.2
  114.2 1.6 copy.18
  115.8 1.1 fusion.60
  117.6 1.4 fusion.73
  119.0 2.2 fusion.84
  121.3 1.3 slice.141
  122.7 0.7 fusion.14
  123.6 1.7 fusion.93
  125.2 1.0 slice.139
  126.3 1.2 convolution_bitcast_fusion.1
  127.5 1.6 copy.23
  129.2 1.1 fusion.51
  130.9 1.4 fusion.75
  132.3 2.2 fusion.83
  134.6 1.2 slice.147
  135.9 0.7 fusion.12
  137.3 1.1 fusion.85
  138.4 1.0 slice.145
  139.4 1.2 convolution_bitcast_fusion
  140.6 1.6 copy.28
  142.2 1.1 fusion.42
  143.4 1.4 fusion.77
  145.0 0.9 copy-done.8
  146.7 0.7 copy-done.3
  152.0 1.6 collective-permute-start.10
  153.6 1.8 collective-permute-done.12
  155.9 1.6 collective-permute-start.13
  157.5 12.8 %collective-permute-done.10 = bf16[168,2048]{1,0:T(8,128)(2,1)S(1)} collective-permute-done((bf16[168,2048]{1,0:T(8,128)(2,1)S(1)}, bf16[168,2048]{1,0:T(8,128)(2,1)S(1)}, u32[]{:S(2)}, u32[]{:S(2)}) %collective-permute-start.10) | collective-permute-done | bytes 688160 | tf_op jit(solution)/shard_map/ppermute | solution.py:31
  171.2 1.6 collective-permute-start.16
  172.8 12.2 %collective-permute-done.13 = bf16[168,2048]{1,0:T(8,128)(2,1)S(1)} collective-permute-done((bf16[168,2048]{1,0:T(8,128)(2,1)S(1)}, bf16[168,2048]{1,0:T(8,128)(2,1)S(1)}, u32[]{:S(2)}, u32[]{:S(2)}) %collective-permute-start.13) | collective-permute-done | bytes 688160 | tf_op jit(solution)/shard_map/ppermute | solution.py:31
  185.0 4.7 %collective-permute-done.11 = bf16[168,2048]{1,0:T(8,128)(2,1)S(1)} collective-permute-done((bf16[168,2048]{1,0:T(8,128)(2,1)S(1)}, bf16[168,2048]{1,0:T(8,128)(2,1)S(1)}, u32[]{:S(2)}, u32[]{:S(2)}) %collective-permute-start.11) | collective-permute-done | bytes 688160 | tf_op jit(solution)/shard_map/ppermute | solution.py:21
  192.2 0.8 collective-permute-start.18
  193.0 6.8 %collective-permute-done.16 = bf16[168,2048]{1,0:T(8,128)(2,1)S(1)} collective-permute-done((bf16[168,2048]{1,0:T(8,128)(2,1)S(1)}, bf16[168,2048]{1,0:T(8,128)(2,1)S(1)}, u32[]{:S(2)}, u32[]{:S(2)}) %collective-permute-start.16) | collective-permute-done | bytes 688160 | tf_op jit(solution)/shard_map/ppermute | solution.py:31
  199.8 8.4 %collective-permute-done.14 = bf16[168,2048]{1,0:T(8,128)(2,1)S(1)} collective-permute-done((bf16[168,2048]{1,0:T(8,128)(2,1)S(1)}, bf16[168,2048]{1,0:T(8,128)(2,1)S(1)}, u32[]{:S(2)}, u32[]{:S(2)}) %collective-permute-start.14) | collective-permute-done | bytes 688160 | tf_op jit(solution)/shard_map/ppermute | solution.py:21
  208.6 1.3 fusion.10
  210.0 15.8 %collective-permute-done.17 = bf16[168,2048]{1,0:T(8,128)(2,1)S(1)} collective-permute-done((bf16[168,2048]{1,0:T(8,128)(2,1)S(1)}, bf16[168,2048]{1,0:T(8,128)(2,1)S(1)}, u32[]{:S(2)}, u32[]{:S(2)}) %collective-permute-start.17) | collective-permute-done | bytes 688160 | tf_op jit(solution)/shard_map/ppermute | solution.py:21
  225.8 1.8 multiply_convert_fusion
  227.5 1.6 collective-permute-start.21
  229.1 1.9 fusion.9
  231.1 10.1 %collective-permute-done.21 = bf16[168,2048]{1,0:T(8,128)(2,1)S(1)} collective-permute-done((bf16[168,2048]{1,0:T(8,128)(2,1)S(1)}, bf16[168,2048]{1,0:T(8,128)(2,1)S(1)}, u32[]{:S(2)}, u32[]{:S(2)}) %collective-permute-start.21) | collective-permute-done | bytes 688160 | tf_op jit(solution)/shard_map/ppermute | solution.py:31
  241.7 1.1 fusion.88
  (138 shorter events, 15.0 us)
Async XLA Ops:
  0.6 2.2 copy-start.30
  2.9 30.7 %copy-start = (bf16[160,4096]{1,0:T(8,128)(2,1)S(1)}, bf16[160,4096]{1,0:T(8,128)(2,1)}, u32[]{:S(2)}) copy-start(bf16[160,4096]{1,0:T(8,128)(2,1)} %param.8) | copy-start | bytes 3932164
  2.9 20.7 %collective-permute-start = (bf16[168,2048]{1,0:T(8,128)(2,1)S(1)}, bf16[168,2048]{1,0:T(8,128)(2,1)}, u32[]{:S(2)}, u32[]{:S(2)}) collective-permute-start(bf16[168,2048]{1,0:T(8,128)(2,1)S(1)} %constant_dynamic-slice_fusion.1), channel_id=1, source_target_pairs={{0,28},{2,30},{4,0},{6,2},{8,4},{10,6},{12,8},{14,10},{16,12},{18,... | collective-permute-start | bytes 2064392 | tf_op jit(solution)/shard_map/ppermute | solution.py:21
  23.7 19.4 %collective-permute-start.3 = (bf16[168,2048]{1,0:T(8,128)(2,1)}, bf16[168,2048]{1,0:T(8,128)(2,1)S(1)}, u32[]{:S(2)}, u32[]{:S(2)}) collective-permute-start(bf16[168,2048]{1,0:T(8,128)(2,1)} %collective-permute-done), channel_id=1, source_target_pairs={{0,28},{2,30},{4,0},{6,2},{8,4},{10,6},{12,8},{14,10},{16,12},{18,... | collective-permute-start | bytes 2064392 | tf_op jit(solution)/shard_map/ppermute | solution.py:21
  31.5 52.0 %collective-permute-start.19 = (f32[168,2048]{1,0:T(8,128)}, f32[168,2048]{1,0:T(8,128)}, u32[]{:S(2)}, u32[]{:S(2)}) collective-permute-start(f32[168,2048]{1,0:T(8,128)} %constant_dynamic-slice_fusion), channel_id=1, source_target_pairs={{0,1},{1,0},{2,3},{3,2},{4,5},{5,4},{6,7},{7,6},{8,9},{9,8},{10,11... | collective-permute-start | bytes 4128776 | tf_op jit(solution)/shard_map/ppermute | solution.py:31
  33.1 46.7 %collective-permute-start.1 = (bf16[168,2048]{1,0:T(8,128)(2,1)}, bf16[168,2048]{1,0:T(8,128)(2,1)}, u32[]{:S(2)}, u32[]{:S(2)}) collective-permute-start(bf16[168,2048]{1,0:T(8,128)(2,1)} %collective-permute-done), channel_id=1, source_target_pairs={{0,1},{1,0},{2,3},{3,2},{4,5},{5,4},{6,7},{7,6},{8,9},{9,8},{10,11... | collective-permute-start | bytes 2064392 | tf_op jit(solution)/shard_map/ppermute | solution.py:31
  33.6 50.0 %copy-start.21 = (f32[3,56,4096]{2,1,0:T(8,128)S(1)}, f32[3,56,4096]{2,1,0:T(8,128)}, u32[]{:S(2)}) copy-start(f32[3,56,4096]{2,1,0:T(8,128)} %param.11) | copy-start | bytes 8257540
  43.1 38.9 %collective-permute-start.6 = (bf16[168,2048]{1,0:T(8,128)(2,1)S(1)}, bf16[168,2048]{1,0:T(8,128)(2,1)S(1)}, u32[]{:S(2)}, u32[]{:S(2)}) collective-permute-start(bf16[168,2048]{1,0:T(8,128)(2,1)S(1)} %collective-permute-done.3), channel_id=1, source_target_pairs={{0,28},{2,30},{4,0},{6,2},{8,4},{10,6},{12,8},{14,10},{16,12},{18,... | collective-permute-start | bytes 2064392 | tf_op jit(solution)/shard_map/ppermute | solution.py:21
  48.7 60.9 %copy-start.34 = (f32[160]{0:T(256)}, f32[160]{0:T(256)S(1)}, u32[]{:S(2)}) copy-start(f32[160]{0:T(256)S(1)} %get-tuple-element.34) | copy-start | bytes 1924
  48.7 45.6 %collective-permute-start.4 = (bf16[168,2048]{1,0:T(8,128)(2,1)S(1)}, bf16[168,2048]{1,0:T(8,128)(2,1)S(1)}, u32[]{:S(2)}, u32[]{:S(2)}) collective-permute-start(bf16[168,2048]{1,0:T(8,128)(2,1)S(1)} %collective-permute-done.3), channel_id=1, source_target_pairs={{0,1},{1,0},{2,3},{3,2},{4,5},{5,4},{6,7},{7,6},{8,9},{9,8},{10,11... | collective-permute-start | bytes 2064392 | tf_op jit(solution)/shard_map/ppermute | solution.py:31
  81.9 27.6 %collective-permute-start.2 = (bf16[168,4096]{1,0:T(8,128)(2,1)S(1)}, bf16[168,4096]{1,0:T(8,128)(2,1)S(1)}, u32[]{:S(2)}, u32[]{:S(2)}) collective-permute-start(bf16[168,4096]{1,0:T(8,128)(2,1)S(1)} %maximum_select_fusion), channel_id=1, source_target_pairs={{0,2},{2,0},{4,6},{6,4},{8,10},{10,8},{12,14},{14,12},{16,18},{18,... | collective-permute-start | bytes 4128776 | tf_op jit(solution)/shard_map/ppermute | solution.py:26
  82.0 24.8 %collective-permute-start.7 = (bf16[168,2048]{1,0:T(8,128)(2,1)S(1)}, bf16[168,2048]{1,0:T(8,128)(2,1)S(1)}, u32[]{:S(2)}, u32[]{:S(2)}) collective-permute-start(bf16[168,2048]{1,0:T(8,128)(2,1)S(1)} %collective-permute-done.6), channel_id=1, source_target_pairs={{0,1},{1,0},{2,3},{3,2},{4,5},{5,4},{6,7},{7,6},{8,9},{9,8},{10,11... | collective-permute-start | bytes 2064392 | tf_op jit(solution)/shard_map/ppermute | solution.py:31
  86.3 23.3 %copy-start.9 = (bf16[112,4096]{1,0:T(8,128)(2,1)}, bf16[112,4096]{1,0:T(8,128)(2,1)S(1)}, u32[]{:S(2)}) copy-start(bf16[112,4096]{1,0:T(8,128)(2,1)S(1)} %slice.134) | copy-start | bytes 2752516
  86.4 123.6 %collective-permute-start.20 = (f32[168,2048]{1,0:T(8,128)}, f32[168,2048]{1,0:T(8,128)}, u32[]{:S(2)}, u32[]{:S(2)}) collective-permute-start(f32[168,2048]{1,0:T(8,128)} %dynamic-slice_add_fusion), channel_id=1, source_target_pairs={{0,12},{2,14},{4,16},{6,18},{8,20},{10,22},{12,24},{14,26},{16,28}... | collective-permute-start | bytes 4128776 | tf_op jit(solution)/shard_map/ppermute | solution.py:21
  96.0 25.3 %collective-permute-start.5 = (bf16[168,4096]{1,0:T(8,128)(2,1)}, bf16[168,4096]{1,0:T(8,128)(2,1)}, u32[]{:S(2)}, u32[]{:S(2)}) collective-permute-start(bf16[168,4096]{1,0:T(8,128)(2,1)} %maximum_select_fusion.1), channel_id=1, source_target_pairs={{0,2},{2,0},{4,6},{6,4},{8,10},{10,8},{12,14},{14,12},{16,18},{18,... | collective-permute-start | bytes 4128776 | tf_op jit(solution)/shard_map/ppermute | solution.py:26
  108.6 27.2 %copy-start.15 = (bf16[112,4096]{1,0:T(8,128)(2,1)}, bf16[112,4096]{1,0:T(8,128)(2,1)S(1)}, u32[]{:S(2)}) copy-start(bf16[112,4096]{1,0:T(8,128)(2,1)S(1)} %slice.146) | copy-start | bytes 2752516
  108.7 1.0 copy-start.33
  109.5 25.0 %collective-permute-start.8 = (bf16[168,4096]{1,0:T(8,128)(2,1)}, bf16[168,4096]{1,0:T(8,128)(2,1)}, u32[]{:S(2)}, u32[]{:S(2)}) collective-permute-start(bf16[168,4096]{1,0:T(8,128)(2,1)} %get-tuple-element.4), channel_id=1, source_target_pairs={{0,2},{2,0},{4,6},{6,4},{8,10},{10,8},{12,14},{14,12},{16,18},{18,... | collective-permute-start | bytes 4128776 | tf_op jit(solution)/shard_map/ppermute | solution.py:26
  109.6 0.9 copy-start.11
  109.7 1.6 copy-start.1
  110.5 2.4 copy-start.28
  116.9 0.7 copy-start.23
  121.3 1.5 copy-start.13
  121.3 1.5 copy-start.35
  122.7 3.6 %copy-start.17 = (bf16[112,4096]{1,0:T(8,128)(2,1)}, bf16[112,4096]{1,0:T(8,128)(2,1)S(1)}, u32[]{:S(2)}) copy-start(bf16[112,4096]{1,0:T(8,128)(2,1)S(1)} %slice.141) | copy-start | bytes 2752516
  123.5 1.8 copy-start.29
  123.6 2.8 %copy-start.32 = (bf16[56,4096]{1,0:T(8,128)(2,1)S(1)}, bf16[56,4096]{1,0:T(8,128)(2,1)}, u32[]{:S(2)}) copy-start(bf16[56,4096]{1,0:T(8,128)(2,1)} %slice.138) | copy-start | bytes 1376260
  130.3 0.6 copy-start.25
  134.6 1.3 copy-start.36
  135.8 0.9 copy-start.19
  136.6 0.7 copy-start.27
  137.3 2.1 copy-start.31
  144.8 1.2 copy-start.8
  146.0 1.5 copy-start.3
  146.2 1.9 copy-start.7
  146.2 5.3 %collective-permute-start.9 = (f32[168,4096]{1,0:T(8,128)S(1)}, f32[168,4096]{1,0:T(8,128)S(1)}, u32[]{:S(2)}, u32[]{:S(2)}) collective-permute-start(f32[168,4096]{1,0:T(8,128)S(1)} %pad_maximum_fusion), channel_id=1, source_target_pairs={{0,2},{2,0},{4,6},{6,4},{8,10},{10,8},{12,14},{14,12},{16,18},{18,... | collective-permute-start | bytes 8257544 | tf_op jit(solution)/shard_map/ppermute | solution.py:26
  148.1 1.5 copy-start.2
  148.3 1.9 copy-start.5
  148.3 7.1 %collective-permute-start.12 = (f32[168,4096]{1,0:T(8,128)S(1)}, f32[168,4096]{1,0:T(8,128)S(1)}, u32[]{:S(2)}, u32[]{:S(2)}) collective-permute-start(f32[168,4096]{1,0:T(8,128)S(1)} %pad_maximum_fusion.1), channel_id=1, source_target_pairs={{0,2},{2,0},{4,6},{6,4},{8,10},{10,8},{12,14},{14,12},{16,18},{18,... | collective-permute-start | bytes 8257544 | tf_op jit(solution)/shard_map/ppermute | solution.py:26
  150.4 20.3 %collective-permute-start.15 = (f32[168,4096]{1,0:T(8,128)S(1)}, f32[168,4096]{1,0:T(8,128)S(1)}, u32[]{:S(2)}, u32[]{:S(2)}) collective-permute-start(f32[168,4096]{1,0:T(8,128)S(1)} %pad_maximum_fusion.2), channel_id=1, source_target_pairs={{0,2},{2,0},{4,6},{6,4},{8,10},{10,8},{12,14},{14,12},{16,18},{18,... | collective-permute-start | bytes 8257544 | tf_op jit(solution)/shard_map/ppermute | solution.py:26
  151.5 3.9 %copy-start.6 = (f32[112,4096]{1,0:T(8,128)S(1)}, f32[112,4096]{1,0:T(8,128)}, u32[]{:S(2)}) copy-start(f32[112,4096]{1,0:T(8,128)} %get-tuple-element.8) | copy-start | bytes 5505028
  152.0 18.3 %collective-permute-start.10 = (bf16[168,2048]{1,0:T(8,128)(2,1)S(1)}, bf16[168,2048]{1,0:T(8,128)(2,1)S(1)}, u32[]{:S(2)}, u32[]{:S(2)}) collective-permute-start(bf16[168,2048]{1,0:T(8,128)(2,1)S(1)} %dynamic-slice_convert_fusion.3), channel_id=1, source_target_pairs={{0,1},{1,0},{2,3},{3,2},{4,5},{5,4},{6,7},{7,6},{8,9},{9,8},{10,11... | collective-permute-start | bytes 2064392 | tf_op jit(solution)/shard_map/ppermute | solution.py:31
  155.8 15.0 %copy-start.4 = (f32[112,4096]{1,0:T(8,128)S(1)}, f32[112,4096]{1,0:T(8,128)}, u32[]{:S(2)}) copy-start(f32[112,4096]{1,0:T(8,128)} %get-tuple-element.10) | copy-start | bytes 5505028
  155.9 29.2 %collective-permute-start.13 = (bf16[168,2048]{1,0:T(8,128)(2,1)S(1)}, bf16[168,2048]{1,0:T(8,128)(2,1)S(1)}, u32[]{:S(2)}, u32[]{:S(2)}) collective-permute-start(bf16[168,2048]{1,0:T(8,128)(2,1)S(1)} %dynamic-slice_convert_fusion.2), channel_id=1, source_target_pairs={{0,1},{1,0},{2,3},{3,2},{4,5},{5,4},{6,7},{7,6},{8,9},{9,8},{10,11... | collective-permute-start | bytes 2064392 | tf_op jit(solution)/shard_map/ppermute | solution.py:31
  170.5 19.3 %collective-permute-start.11 = (bf16[168,2048]{1,0:T(8,128)(2,1)S(1)}, bf16[168,2048]{1,0:T(8,128)(2,1)S(1)}, u32[]{:S(2)}, u32[]{:S(2)}) collective-permute-start(bf16[168,2048]{1,0:T(8,128)(2,1)S(1)} %add_convert_fusion.2), channel_id=1, source_target_pairs={{0,4},{2,6},{4,8},{6,10},{8,12},{10,14},{12,16},{14,18},{16,20},{1... | collective-permute-start | bytes 2064392 | tf_op jit(solution)/shard_map/ppermute | solution.py:21
  171.2 18.9 %copy-start.14 = (bf16[112,4096]{1,0:T(8,128)(2,1)S(1)}, bf16[112,4096]{1,0:T(8,128)(2,1)}, u32[]{:S(2)}) copy-start(bf16[112,4096]{1,0:T(8,128)(2,1)} %slice.140) | copy-start | bytes 2752516
  171.2 18.9 %copy-start.18 = (bf16[112,4096]{1,0:T(8,128)(2,1)S(1)}, bf16[112,4096]{1,0:T(8,128)(2,1)}, u32[]{:S(2)}) copy-start(bf16[112,4096]{1,0:T(8,128)(2,1)} %copy-done.17) | copy-start | bytes 2752516
  171.2 18.9 %copy-start.26 = (bf16[160,2,2,56]{0,3,2,1:T(8,128)(2,1)S(1)}, bf16[160,2,2,56]{0,3,2,1:T(8,128)(2,1)}, u32[]{:S(2)}) copy-start(bf16[160,2,2,56]{0,3,2,1:T(8,128)(2,1)} %copy-done.25) | copy-start | bytes 215044
  171.2 28.6 %collective-permute-start.16 = (bf16[168,2048]{1,0:T(8,128)(2,1)S(1)}, bf16[168,2048]{1,0:T(8,128)(2,1)S(1)}, u32[]{:S(2)}, u32[]{:S(2)}) collective-permute-start(bf16[168,2048]{1,0:T(8,128)(2,1)S(1)} %dynamic-slice_convert_fusion.1), channel_id=1, source_target_pairs={{0,1},{1,0},{2,3},{3,2},{4,5},{5,4},{6,7},{7,6},{8,9},{9,8},{10,11... | collective-permute-start | bytes 2064392 | tf_op jit(solution)/shard_map/ppermute | solution.py:31
  190.0 1.2 copy-start.16
  190.0 1.4 copy-start.20
  190.0 18.2 %collective-permute-start.14 = (bf16[168,2048]{1,0:T(8,128)(2,1)S(1)}, bf16[168,2048]{1,0:T(8,128)(2,1)S(1)}, u32[]{:S(2)}, u32[]{:S(2)}) collective-permute-start(bf16[168,2048]{1,0:T(8,128)(2,1)S(1)} %add_convert_fusion.1), channel_id=1, source_target_pairs={{0,4},{2,6},{4,8},{6,10},{8,12},{10,14},{12,16},{14,18},{16,20},{1... | collective-permute-start | bytes 2064392 | tf_op jit(solution)/shard_map/ppermute | solution.py:21
  192.0 16.6 %copy-start.22 = (f32[160,4096]{1,0:T(8,128)S(1)}, f32[160,4096]{1,0:T(8,128)}, u32[]{:S(2)}) copy-start(f32[160,4096]{1,0:T(8,128)} %param.10) | copy-start | bytes 7864324
  192.1 16.5 %copy-start.10 = (bf16[112,4096]{1,0:T(8,128)(2,1)S(1)}, bf16[112,4096]{1,0:T(8,128)(2,1)}, u32[]{:S(2)}) copy-start(bf16[112,4096]{1,0:T(8,128)(2,1)} %copy-done.9) | copy-start | bytes 2752516
  192.1 16.5 %copy-start.12 = (bf16[112,4096]{1,0:T(8,128)(2,1)S(1)}, bf16[112,4096]{1,0:T(8,128)(2,1)}, u32[]{:S(2)}) copy-start(bf16[112,4096]{1,0:T(8,128)(2,1)} %copy-done.11) | copy-start | bytes 2752516
  192.2 16.5 %copy-start.24 = (bf16[160,2,2,56]{0,3,2,1:T(8,128)(2,1)S(1)}, bf16[160,2,2,56]{0,3,2,1:T(8,128)(2,1)}, u32[]{:S(2)}) copy-start(bf16[160,2,2,56]{0,3,2,1:T(8,128)(2,1)} %copy-done.23) | copy-start | bytes 215044
  192.2 17.8 %collective-permute-start.18 = (bf16[168,2048]{1,0:T(8,128)(2,1)S(1)}, bf16[168,2048]{1,0:T(8,128)(2,1)S(1)}, u32[]{:S(2)}, u32[]{:S(2)}) collective-permute-start(bf16[168,2048]{1,0:T(8,128)(2,1)S(1)} %dynamic-slice_convert_fusion), channel_id=1, source_target_pairs={{2,3},{3,2},{6,7},{7,6},{10,11},{11,10},{14,15},{15,14},{18,19},{1... | collective-permute-start | bytes 2064392 | tf_op jit(solution)/shard_map/ppermute | solution.py:41
  208.5 17.2 %collective-permute-start.17 = (bf16[168,2048]{1,0:T(8,128)(2,1)S(1)}, bf16[168,2048]{1,0:T(8,128)(2,1)S(1)}, u32[]{:S(2)}, u32[]{:S(2)}) collective-permute-start(bf16[168,2048]{1,0:T(8,128)(2,1)S(1)} %add_convert_fusion), channel_id=1, source_target_pairs={{0,4},{2,6},{4,8},{6,10},{8,12},{10,14},{12,16},{14,18},{16,20},{1... | collective-permute-start | bytes 2064392 | tf_op jit(solution)/shard_map/ppermute | solution.py:21
  209.9 19.2 %copy-start.37 = (f32[160]{0:T(256)S(1)}, f32[160]{0:T(256)}, u32[]{:S(2)}) copy-start(f32[160]{0:T(256)} %copy-done.34) | copy-start | bytes 1924
  209.9 19.2 %copy-start.38 = (f32[160]{0:T(256)S(1)}, f32[160]{0:T(256)}, u32[]{:S(2)}) copy-start(f32[160]{0:T(256)} %get-tuple-element.33) | copy-start | bytes 1924
  227.5 13.6 %collective-permute-start.21 = (bf16[168,2048]{1,0:T(8,128)(2,1)S(1)}, bf16[168,2048]{1,0:T(8,128)(2,1)S(1)}, u32[]{:S(2)}, u32[]{:S(2)}) collective-permute-start(bf16[168,2048]{1,0:T(8,128)(2,1)S(1)} %multiply_convert_fusion), channel_id=1, source_target_pairs={{0,1},{1,0},{2,3},{3,2},{4,5},{5,4},{6,7},{7,6},{8,9},{9,8},{10,11... | collective-permute-start | bytes 2064392 | tf_op jit(solution)/shard_map/ppermute | solution.py:31

commit v2 on v1

v2 whole, which is shorter than its diff:
```python
import math

import jax
import jax.numpy as jnp
from jax import lax
from jax.experimental import pallas as pl
from jax.experimental.pallas import tpu as pltpu
from jax.sharding import PartitionSpec as P

CYCLE_STEPS = 6
CORES = 2
HOPS = CYCLE_STEPS // CORES

CHAIN = jnp.bfloat16
REP = jnp.bfloat16
SWAP = jnp.float32

epsilon = 1e-05
SPLIT = 2
ROWS16 = 16
MESH = pl.DeviceIdType.MESH


def moved(value, steps):
    count = lax.axis_size("blk")
    return lax.ppermute(value, "blk", [(i, (i + steps) % count) for i in range(count)])


def swapped_core(value):
    count = lax.axis_size("blk")
    return lax.ppermute(value, "blk", [(i, i ^ 1) for i in range(count)])


def swapped_rep(value):
    count = lax.axis_size("rep")
    return lax.ppermute(value, "rep", [(i, (i + 1) % count) for i in range(count)])


def swapped_rep_upper(value):
    reps = lax.axis_size("rep")
    pairs = [
        (i * reps + r, i * reps + (r + 1) % reps)
        for i in range(1, lax.axis_size("blk"), CORES)
        for r in range(reps)
    ]
    return lax.ppermute(value, ("blk", "rep"), pairs)


def gather_kernel(
    chips, w_ref, mine_ref, theirs_ref, out_ref, held_ref, home_buf, twin_buf,
    ring_send, ring_recv, rep_send, rep_recv, core_send, core_recv, swap_sem, home_sem,
):
    blk = lax.axis_index("blk")
    rep = lax.axis_index("rep")
    core = lax.rem(blk, CORES)
    count = chips * CORES
    odd = lax.rem(blk // CORES, 2)
    before = (lax.rem(blk + count - 2 * CORES, count), rep)
    after = (lax.rem(blk + 2 * CORES, count), rep)
    beside = (blk + CORES * (1 - 2 * odd), rep)
    sibling = (blk + 1 - 2 * core, rep)
    twin = (blk, 1 - rep)
    ahead = (lax.rem(blk + CYCLE_STEPS, count), rep)
    behind = (lax.rem(blk + count - CYCLE_STEPS, count), rep)
    part = w_ref.shape[1] // (2 * SPLIT)

    barrier = pltpu.get_barrier_semaphore()
    for peer in (before, after, beside, sibling, twin, ahead, behind):
        pl.semaphore_signal(barrier, inc=1, device_id=peer, device_id_type=MESH)
    pl.semaphore_wait(barrier, 7)

    def lanes(owner, s):
        return pl.ds(pl.multiple_of((owner * SPLIT + s) * part, part), part)

    def ring(j, s, src, target, out=None):
        return pltpu.make_async_remote_copy(
            src_ref=src.at[:, lanes(rep, s)],
            dst_ref=out_ref.at[2 * j].at[:, lanes(rep, s)],
            send_sem=ring_send.at[j if out is None else out, s],
            recv_sem=ring_recv.at[j, s],
            device_id=target,
            device_id_type=MESH,
        )

    def to_twin(j, s, owner):
        return pltpu.make_async_remote_copy(
            src_ref=out_ref.at[2 * j].at[:, lanes(owner, s)],
            dst_ref=out_ref.at[2 * j].at[:, lanes(owner, s)],
            send_sem=rep_send.at[j, s],
            recv_sem=rep_recv.at[j, s],
            device_id=twin,
            device_id_type=MESH,
        )

    def to_sibling(j, s, owner, side, src):
        return pltpu.make_async_remote_copy(
            src_ref=src.at[:, lanes(owner, s)],
            dst_ref=out_ref.at[2 * j + 1].at[:, lanes(owner, s)],
            send_sem=core_send.at[j, s, side],
            recv_sem=core_recv.at[j, s, side],
            device_id=sibling,
            device_id_type=MESH,
        )

    last = HOPS - 1

    def pass_to_sibling(j, s, owner, side):
        if j < last:
            to_sibling(j, s, owner, side, out_ref.at[2 * j]).start()
        else:
            @pl.when(core == 0)
            def _():
                to_sibling(j, s, owner, side, out_ref.at[2 * j]).start()

    swap = pltpu.make_async_remote_copy(
        src_ref=theirs_ref,
        dst_ref=twin_buf,
        send_sem=swap_sem.at[0],
        recv_sem=swap_sem.at[1],
        device_id=twin,
        device_id_type=MESH,
    )
    home = pltpu.make_async_remote_copy(
        src_ref=home_buf,
        dst_ref=held_ref,
        send_sem=home_sem.at[0],
        recv_sem=home_sem.at[1],
        device_id=ahead,
        device_id_type=MESH,
    )
    swap.start()
    for s in range(SPLIT):
        ring(1, s, w_ref, before).start()

    @pl.when(odd == 1)
    def _():
        for s in range(SPLIT):
            ring(0, s, w_ref, beside).start()

    @pl.when(core == 1)
    def _():
        for s in range(SPLIT):
            for side, owner in enumerate((rep, 1 - rep)):
                to_sibling(last, s, owner, side, w_ref).start()

    def on_ring(j):
        for s in range(SPLIT):
            ring(j, s, w_ref, before).wait_recv()
            if j == 1:
                @pl.when(odd == 1)
                def _():
                    ring(2, s, out_ref.at[2], beside).start()

                @pl.when(odd == 0)
                def _():
                    ring(0, s, out_ref.at[2], beside).start()
            if j == 0:
                @pl.when(odd == 1)
                def _():
                    ring(2, s, out_ref.at[0], before, HOPS).start()
            to_twin(j, s, rep).start()
            pass_to_sibling(j, s, rep, 0)

    def on_twin(j):
        for s in range(SPLIT):
            to_twin(j, s, 1 - rep).wait_recv()
            pass_to_sibling(j, s, 1 - rep, 1)

    on_ring(1)
    swap.wait()

    def add(i, _):
        at = pl.ds(pl.multiple_of(i * ROWS16, ROWS16), ROWS16)
        total = mine_ref[at, :] + twin_buf[at, :].astype(jnp.float32)
        home_buf[at, :] = total.astype(home_buf.dtype)
        return _

    lax.fori_loop(0, mine_ref.shape[0] // ROWS16, add, 0)
    home.start()
    on_ring(0)
    on_twin(1)
    on_ring(2)
    on_twin(0)
    on_twin(2)
    for j in range(HOPS):
        for s in range(SPLIT):
            if j < 2:
                ring(j, s, w_ref, before).wait_send()
            to_twin(j, s, rep).wait_send()
            for side, owner in enumerate((rep, 1 - rep)):
                copy = to_sibling(j, s, owner, side, w_ref)
                copy.wait_send()
                copy.wait_recv()
    home.wait()

    @pl.when(odd == 1)
    def _():
        for s in range(SPLIT):
            ring(2, s, w_ref, beside).wait_send()
            ring(2, s, w_ref, before, HOPS).wait_send()


def gathered(own_weights, mine, theirs):
    rows, width = own_weights.shape
    chips = lax.axis_size("blk") // CORES
    return pl.pallas_call(
        lambda *refs: gather_kernel(chips, *refs),
        out_shape=(
            jax.ShapeDtypeStruct((2 * HOPS, rows, width), own_weights.dtype),
            jax.ShapeDtypeStruct(theirs.shape, theirs.dtype),
        ),
        in_specs=[
            pl.BlockSpec(memory_space=pl.ANY),
            pl.BlockSpec(memory_space=pltpu.VMEM),
            pl.BlockSpec(memory_space=pl.ANY),
        ],
        out_specs=(pl.BlockSpec(memory_space=pl.ANY),) * 2,
        scratch_shapes=[
            pltpu.VMEM(mine.shape, theirs.dtype),
            pltpu.VMEM(mine.shape, theirs.dtype),
            pltpu.SemaphoreType.DMA((HOPS + 1, SPLIT)),
            pltpu.SemaphoreType.DMA((HOPS, SPLIT)),
            pltpu.SemaphoreType.DMA((HOPS, SPLIT)),
            pltpu.SemaphoreType.DMA((HOPS, SPLIT)),
            pltpu.SemaphoreType.DMA((HOPS, SPLIT, 2)),
            pltpu.SemaphoreType.DMA((HOPS, SPLIT, 2)),
            pltpu.SemaphoreType.DMA((2,)),
            pltpu.SemaphoreType.DMA((2,)),
        ],
        compiler_params=pltpu.CompilerParams(
            collective_id=0, has_side_effects=True, vmem_limit_bytes=16 * 2**20
        ),
        name="gather_weights",
    )(own_weights, mine, theirs)


def group_terms(normed, grad_in, groups, units):
    tokens, width = normed.shape
    count, rows, _ = groups.shape
    flat = groups.reshape(count * rows, width)
    left = jnp.einsum("td,fd->tf", normed, flat, preferred_element_type=jnp.float32)
    right = jnp.einsum("td,fd->tf", grad_in, flat, preferred_element_type=jnp.float32)
    left = left.reshape(tokens, count, rows)
    gate, upper = left[:, :, :units], left[:, :, units : 2 * units]
    dhidden = right.reshape(tokens, count, rows)[:, :, 2 * units : 3 * units]
    sigma = jax.nn.sigmoid(gate)
    act = gate * sigma
    hidden = (act * upper).astype(jnp.bfloat16)
    dgate = (dhidden * upper * sigma * (1.0 + gate * (1.0 - sigma))).astype(jnp.bfloat16)
    dup = (dhidden * act).astype(jnp.bfloat16)
    rest = rows - 2 * units
    dgu = jnp.pad(jnp.concatenate([dgate, dup], axis=2), ((0, 0), (0, 0), (0, rest)))
    dgu = dgu.reshape(tokens, count * rows)
    hid = jnp.pad(hidden, ((0, 0), (0, 0), (2 * units, rest - units)))
    hid = hid.reshape(tokens, count * rows)
    dnormed = jnp.einsum("tf,fd->td", dgu, flat, preferred_element_type=jnp.float32)
    terms = jnp.einsum(
        "tf,td->fd",
        jnp.concatenate([dgu, hid], axis=0),
        jnp.concatenate([normed, grad_in], axis=0),
        preferred_element_type=jnp.float32,
    )
    return terms.reshape(count, rows, width), dnormed


def shards(block_inputs, out_cotangent, dnormed_in, carried_sums, norm_gain, w_gate, w_up, w_down):
    reps = lax.axis_size("rep")
    scale = 1.0 / math.sqrt(lax.axis_size("blk") * block_inputs.shape[0] * reps)
    core = lax.rem(lax.axis_index("blk"), CORES)
    rep = lax.axis_index("rep")
    units, width = w_gate.shape
    half = width // 2

    def mine(v):
        return lax.dynamic_slice_in_dim(v, rep * half, half, axis=v.ndim - 1)

    def theirs(v):
        return lax.dynamic_slice_in_dim(v, (1 - rep) * half, half, axis=v.ndim - 1)

    def joined(a, b):
        return jnp.where(rep == 0, jnp.concatenate([a, b], -1), jnp.concatenate([b, a], -1))

    def summed(v):
        return mine(v) + swapped_rep(theirs(v).astype(REP)).astype(jnp.float32)

    spare = jnp.zeros((-3 * units % ROWS16, width), w_gate.dtype)
    carried = jnp.pad(carried_sums.reshape(3 * units, width), ((0, spare.shape[0]), (0, 0)))
    groups, held = gathered(
        jnp.concatenate([w_gate, w_up, w_down, spare], axis=0),
        mine(carried),
        theirs(carried).astype(REP),
    )
    held = held[: 3 * units].astype(jnp.float32)

    values = block_inputs.astype(jnp.float32)
    rstd = lax.rsqrt(jnp.mean(values * values, axis=-1, keepdims=True) + epsilon)
    normed = (values * rstd * norm_gain).astype(jnp.bfloat16)

    terms, part = group_terms(normed, out_cotangent, groups, units)
    terms = terms[:, : 3 * units]
    dnormed = dnormed_in + part
    reduced = []
    for j in range(HOPS):
        own_term, other_term = terms[2 * j], terms[2 * j + 1]
        received = swapped_core(other_term.astype(SWAP)).astype(jnp.float32)
        if j < HOPS - 1:
            reduced.append(own_term + received)
        else:
            last = own_term + jnp.where(core == 0, received, 0.0)
            reduced.append(last)
            near = mine(received) + swapped_rep_upper(theirs(received).astype(REP)).astype(
                jnp.float32
            )
            near = jnp.where(core == 0, 0.0, near)

    sums = summed(reduced[HOPS - 1])
    for j in range(HOPS - 2, -1, -1):
        sums = moved(sums.astype(CHAIN), CORES).astype(jnp.float32) + summed(reduced[j])
    sums = moved(sums.astype(CHAIN), CORES).astype(jnp.float32) + near
    rounded = ((sums + held) * scale).astype(jnp.bfloat16)
    finals = joined(rounded, swapped_rep(rounded))

    scaled = norm_gain * dnormed
    dx = rstd * scaled - values * rstd**3 * jnp.mean(values * scaled, axis=-1, keepdims=True)
    input_grad = (out_cotangent.astype(jnp.float32) + dx).astype(jnp.bfloat16)
    return (input_grad, finals[:units], finals[units : 2 * units], finals[2 * units :])


def solution(mesh):
    placed = (
        P(("blk", "rep"), None),
        P(("blk", "rep"), None),
        P(("blk", "rep"), None),
        P(None, ("blk", "rep"), None),
        P(),
        P("blk", None),
        P("blk", None),
        P("blk", None),
    )
    return jax.shard_map(
        shards,
        mesh=mesh,
        in_specs=placed,
        out_specs=(P(("blk", "rep"), None), P("blk", None), P("blk", None), P("blk", None)),
        check_vma=False,
    )
```

time: 244 us -> 234 us (0.959)
  Pallas kernels: 0 us -> 70.6 us
  waiting for transfers between devices: 141 us -> 72.6 us
  starting transfers between devices: 30.9 us -> 10.5 us
  matrix products: 16.1 us -> 22.6 us
  other arithmetic: 19.3 us -> 22.6 us
    pallas_call x0 -> x1, Pallas kernels: none -> 70.6 us  [gathered(): pl.pallas_call(lambda *refs: gather_kernel(chips, *refs), out_shape=(jax....]
    ppermute x8 -> x4, waiting for transfers between devices: 86.1 us -> 39.9 us  [swapped_rep(): lax.ppermute(value, 'rep', [(i, (i + 1) % count) for i in range(count)])]
    ppermute x7 -> x3, waiting for transfers between devices: 52.8 us -> 20.3 us  [moved(): lax.ppermute(value, 'blk', [(i, (i + steps) % count) for i in range(count)])]
    slice x21 -> x1, local copies, waits for them, and re-layouts: 15.9 us -> 1.55 us  [group_terms(): dhidden = right.reshape(tokens, count, rows)[:, :, 2 * units:3 * units]]
    ppermute x7 -> x3, starting transfers between devices: 16.8 us -> 5.73 us  [moved(): lax.ppermute(value, 'blk', [(i, (i + steps) % count) for i in range(count)])]
    ppermute x6 -> x3, waiting for transfers between devices: 2.32 us -> 12.4 us  [swapped_core(): return lax.ppermute(value, 'blk', [(i, i ^ 1) for i in range(count)])]
    add x1, other arithmetic: 0.4 us -> 10.2 us  [shards(): last = own_term + jnp.where(core == 0, received, 0.0)]
    ppermute x8 -> x4, starting transfers between devices: 11.5 us -> 3.2 us  [swapped_rep(): lax.ppermute(value, 'rep', [(i, (i + 1) % count) for i in range(count)])]
  transfers between devices with their start and end apart: 22 -> 11, of which waited for: 14 -> 10; matrix products, arithmetic and copies ran while one was open for 23% -> 7% of each run, Pallas kernels for 0% -> 0%
where the time goes in v2:
time: 234 us
  waiting for transfers between devices  72.6 us (31%)
  Pallas kernels  70.6 us (30%)
  local copies, waits for them, and re-layouts  33.8 us (14%)
  other arithmetic  22.6 us (10%)
  matrix products  22.6 us (10%)
  starting transfers between devices  10.5 us (4%)
    pallas_call x1, Pallas kernels, gathered(): pl.pallas_call(lambda *refs: gather_kernel(chips, *refs), out_shape=(jax....  70.6 us
    ppermute x4, waiting for transfers between devices, swapped_rep(): lax.ppermute(value, 'rep', [(i, (i + 1) % count) for i in range(count)])  39.9 us
    ppermute x3, waiting for transfers between devices, moved(): lax.ppermute(value, 'blk', [(i, (i + steps) % count) for i in range(count)])  20.3 us
    ppermute x3, waiting for transfers between devices, swapped_core(): return lax.ppermute(value, 'blk', [(i, i ^ 1) for i in range(count)])  12.4 us
    add x1, other arithmetic, shards(): last = own_term + jnp.where(core == 0, received, 0.0)  10.2 us
    unnamed x33, local copies, waits for them, and re-layouts  9.14 us
    dot_general x1, matrix products, group_terms(): jnp.einsum('td,fd->tf', normed, flat, preferred_element_type=jnp.float32)  6.33 us
    dot_general x1, matrix products, group_terms(): jnp.einsum('tf,td->fd', jnp.concatenate([dgu, hid], axis=0), jnp.concaten...  6.25 us
  transfers between devices with their start and end apart: 11, of which 10 were waited for; matrix products, arithmetic and copies ran while one was open for 7% of the time, Pallas kernels for 0%

profile of v2, /device:TPU:0, one launch (start us, length us, event | category | flops | bytes accessed | tf_op | source)
XLA Modules:
  0.0 233.6 jit_solution(6332540865035503055)
XLA Ops:
  0.6 0.0 copy-start.3
  0.7 1.8 fusion.5
  2.5 1.4 fusion.17.refs_2_
  3.9 0.0 copy-start.11
  3.9 0.0 copy-start.12
  3.9 0.0 copy-start.13
  4.0 0.1 pad_dynamic-slice_fusion.1.refs_1_
  4.1 0.1 pad.28.clone
  4.2 0.8 copy-done.11
  4.9 0.1 copy-done.12
  5.1 0.1 copy-done.13
  5.2 0.3 maximum_maximum_fusion.refs_0_
  5.6 70.6 %gather_weights.1 = (bf16[6,176,4096]{2,1,0:T(8,128)(2,1)S(1)}, bf16[176,2048]{1,0:T(8,128)(2,1)S(1)}) custom-call(bf16[176,4096]{1,0:T(8,128)(2,1)S(1)} %maximum_maximum_fusion.refs_0_, f32[176,2048]{1,0:T(8,128)S(1)} %pad_dynamic-slice_fusion.1.refs_1_, bf16[176,2048]{1,0:T(8,128)(2,1)S(1)} %fusion.17.refs_2_), custom_call_target="tpu_custom_call" | custom-call | tf_op jit(solution)/shard_map/gather_weights/pallas_call | solution.py:206
  76.2 3.4 %copy-done = bf16[6,176,4096]{2,1,0:T(8,128)(2,1)} copy-done((bf16[6,176,4096]{2,1,0:T(8,128)(2,1)}, bf16[6,176,4096]{2,1,0:T(8,128)(2,1)S(1)}, u32[]{:S(2)}) %copy-start) | copy-done | bytes 8650776
  79.6 4.1 %convolution_bitcast_fusion.1 = f32[160,1056]{1,0:T(8,128)} fusion(bf16[1056,4096]{1,0:T(8,128)(2,1)S(1)} %bitcast.36, bf16[160,4096]{1,0:T(8,128)(2,1)S(1)} %copy-done.7), kind=kOutput, calls=%fused_computation.30 | convolution fusion | flops 1384120320 | bytes 10637312 | tf_op jit(solution)/shard_map/td,fd->tf/dot_general | solution.py:242
  83.7 3.0 %reshape.50 = f32[160,6,176]{2,1,0:T(8,128)} reshape(f32[160,1056]{1,0:T(8,128)} %convolution_bitcast_fusion.1) | data formatting | bytes 1351680 | tf_op jit(solution)/shard_map/reshape | solution.py:245
  86.7 1.5 slice.59
  88.2 0.4 fusion.7
  88.6 0.0 copy-start.8
  88.6 6.3 %fusion.18 = f32[160,6,176]{2,0,1:T(8,128)S(1)} fusion(bf16[6,176,4096]{2,1,0:T(8,128)(2,1)} %copy-done, bf16[160,4096]{1,0:T(8,128)(2,1)S(1)} %fusion.7), kind=kOutput, calls=%fused_computation.42 | convolution fusion | flops 1384120320 | bytes 10637312 | tf_op jit(solution)/shard_map/td,fd->tf/dot_general | solution.py:241
  95.0 1.1 multiply_convert_fusion.3
  96.1 0.1 copy.17
  96.2 1.1 pad.14.clone
  97.4 2.3 %reshape.52 = bf16[160,1056]{1,0:T(8,128)(2,1)} reshape(bf16[160,6,176]{2,1,0:T(8,128)(2,1)} %pad.14.clone) | data formatting | bytes 675840 | tf_op jit(solution)/shard_map/reshape | solution.py:255
  99.7 1.2 fusion.25
  100.9 1.1 copy.14
  102.1 2.3 %reshape.51 = bf16[160,1056]{1,0:T(8,128)(2,1)} reshape(bf16[160,6,176]{2,1,0:T(8,128)(2,1)} %copy.14) | data formatting | bytes 675840 | tf_op jit(solution)/shard_map/reshape | solution.py:253
  104.4 6.2 %fusion.13 = f32[1056,4096]{1,0:T(8,128)S(1)} fusion(bf16[160,4096]{1,0:T(8,128)(2,1)S(1)} %copy-done.7, bf16[160,4096]{1,0:T(8,128)(2,1)} %copy-done.8, bf16[160,1056]{1,0:T(8,128)(2,1)} %reshape.52, bf16[160,1056]{1,0:T(8,128)(2,1)} %reshape.51), kind=kOutput, calls=%fused_computation.26 | convolution fusion | flops 2774835200 | bytes 20598784 | tf_op jit(solution)/shard_map/tf,td->fd/dot_general | solution.py:257
  110.7 3.9 %slice_bitcast_fusion.2 = (f32[168,4096]{1,0:T(8,128)}, f32[168,4096]{1,0:T(8,128)}, f32[168,4096]{1,0:T(8,128)}) fusion(f32[6,176,4096]{2,1,0:T(8,128)S(1)} %bitcast.37), kind=kLoop, calls=%fused_computation.12 | loop fusion | bytes 16515072 | tf_op jit(solution)/shard_map/squeeze | solution.py:304
  114.6 4.5 %copy-done.1 = f32[1056,4096]{1,0:T(8,128)} copy-done((f32[1056,4096]{1,0:T(8,128)}, f32[1056,4096]{1,0:T(8,128)S(1)}, u32[]{:S(2)}) %copy-start.1) | copy-done | bytes 17301528
  119.1 0.4 collective-permute-start.3
  119.4 0.1 collective-permute-start.6
  119.6 0.4 collective-permute-start
  120.0 4.6 %collective-permute-done.3 = f32[168,4096]{1,0:T(8,128)} collective-permute-done((f32[168,4096]{1,0:T(8,128)}, f32[168,4096]{1,0:T(8,128)}, u32[]{:S(2)}, u32[]{:S(2)}) %collective-permute-start.3) | collective-permute-done | bytes 2752544 | tf_op jit(solution)/shard_map/ppermute | solution.py:31
  124.5 3.9 %collective-permute-done.6 = f32[168,4096]{1,0:T(8,128)} collective-permute-done((f32[168,4096]{1,0:T(8,128)}, f32[168,4096]{1,0:T(8,128)}, u32[]{:S(2)}, u32[]{:S(2)}) %collective-permute-start.6) | collective-permute-done | bytes 2752544 | tf_op jit(solution)/shard_map/ppermute | solution.py:31
  128.5 3.9 %collective-permute-done = f32[168,4096]{1,0:T(8,128)} collective-permute-done((f32[168,4096]{1,0:T(8,128)}, f32[168,4096]{1,0:T(8,128)}, u32[]{:S(2)}, u32[]{:S(2)}) %collective-permute-start) | collective-permute-done | bytes 2752544 | tf_op jit(solution)/shard_map/ppermute | solution.py:31
  132.4 10.2 %fusion.4 = (f32[168,4096]{1,0:T(8,128)}, f32[168,4096]{1,0:T(8,128)S(1)}, f32[168,4096]{1,0:T(8,128)}) fusion(f32[6,176,4096]{2,1,0:T(8,128)} %bitcast.38, f32[168,4096]{1,0:T(8,128)} %collective-permute-done, pred[]{:T(512)S(6)} %eq.8, f32[168,4096]{1,0:T(8,128)} %collective-permute-done.6, f32[168,4096]{1,0:T(8,128)} %collective-permute-done.3), kind=kLoop, calls=%fused_computation.17 | loop fusion | flops 2752512 | bytes 24772608 | tf_op jit(solution)/shard_map/add | solution.py:309
  142.6 2.5 %dynamic-slice_convert_fusion.3 = bf16[168,2048]{1,0:T(8,128)(2,1)S(1)} fusion(f32[168,4096]{1,0:T(8,128)} %get-tuple-element.8, s32[]{:T(128)S(6)} %select_n.39), kind=kLoop, calls=%fused_computation.41 | loop fusion | bytes 1376260 | tf_op jit(solution)/shard_map/convert_element_type | solution.py:284
  145.1 0.6 collective-permute-start.1
  145.7 1.6 dynamic-slice_convert_fusion.2
  147.3 1.6 collective-permute-start.4
  148.9 14.7 %collective-permute-done.1 = bf16[168,2048]{1,0:T(8,128)(2,1)S(1)} collective-permute-done((bf16[168,2048]{1,0:T(8,128)(2,1)S(1)}, bf16[168,2048]{1,0:T(8,128)(2,1)S(1)}, u32[]{:S(2)}, u32[]{:S(2)}) %collective-permute-start.1) | collective-permute-done | bytes 688160 | tf_op jit(solution)/shard_map/ppermute | solution.py:36
  163.5 0.2 add_convert_fusion.2
  163.7 4.5 %collective-permute-start.2 = (bf16[168,2048]{1,0:T(8,128)(2,1)S(1)}, bf16[168,2048]{1,0:T(8,128)(2,1)S(1)}, u32[]{:S(2)}, u32[]{:S(2)}) collective-permute-start(bf16[168,2048]{1,0:T(8,128)(2,1)S(1)} %add_convert_fusion.2), channel_id=1, source_target_pairs={{0,4},{2,6},{4,8},{6,10},{8,12},{10,14},{12,16},{14,18},{16,20},{1... | collective-permute-start | bytes 2064392 | tf_op jit(solution)/shard_map/ppermute | solution.py:26
  168.2 0.9 dynamic-slice_convert_fusion.1
  169.1 0.6 collective-permute-start.7
  169.7 8.6 %collective-permute-done.4 = bf16[168,2048]{1,0:T(8,128)(2,1)S(1)} collective-permute-done((bf16[168,2048]{1,0:T(8,128)(2,1)S(1)}, bf16[168,2048]{1,0:T(8,128)(2,1)S(1)}, u32[]{:S(2)}, u32[]{:S(2)}) %collective-permute-start.4) | collective-permute-done | bytes 688160 | tf_op jit(solution)/shard_map/ppermute | solution.py:36
  178.3 4.1 %collective-permute-done.2 = bf16[168,2048]{1,0:T(8,128)(2,1)S(1)} collective-permute-done((bf16[168,2048]{1,0:T(8,128)(2,1)S(1)}, bf16[168,2048]{1,0:T(8,128)(2,1)S(1)}, u32[]{:S(2)}, u32[]{:S(2)}) %collective-permute-start.2) | collective-permute-done | bytes 688160 | tf_op jit(solution)/shard_map/ppermute | solution.py:26
  182.4 1.2 add_convert_fusion.1
  183.6 0.3 collective-permute-start.5
  183.9 1.6 dynamic-slice_convert_fusion
  185.5 0.7 collective-permute-start.9
  186.2 6.9 %collective-permute-done.7 = bf16[168,2048]{1,0:T(8,128)(2,1)} collective-permute-done((bf16[168,2048]{1,0:T(8,128)(2,1)}, bf16[168,2048]{1,0:T(8,128)(2,1)}, u32[]{:S(2)}, u32[]{:S(2)}) %collective-permute-start.7) | collective-permute-done | bytes 688160 | tf_op jit(solution)/shard_map/ppermute | solution.py:36
  193.1 7.3 %collective-permute-done.5 = bf16[168,2048]{1,0:T(8,128)(2,1)} collective-permute-done((bf16[168,2048]{1,0:T(8,128)(2,1)}, bf16[168,2048]{1,0:T(8,128)(2,1)}, u32[]{:S(2)}, u32[]{:S(2)}) %collective-permute-start.5) | collective-permute-done | bytes 688160 | tf_op jit(solution)/shard_map/ppermute | solution.py:26
  200.5 2.0 add_convert_fusion
  202.5 0.9 collective-permute-start.8
  203.4 5.9 %fusion.12 = (f32[160]{0:T(256)S(1)}, f32[160,4096]{1,0:T(8,128)S(1)}) fusion(bf16[160,4096]{1,0:T(8,128)(2,1)S(1)} %copy-done.2, f32[160,4096]{1,0:T(8,128)S(1)} %copy-done.15, bf16[6,176,4096]{2,1,0:T(8,128)(2,1)} %copy-done, bf16[160,6,56]{2,0,1:T(8,128)(2,1)S(1)} %copy-done.10, bf16[160,6,56]{2,0,1:T(8,128)(2,1)S(1)} %copy-done.9, f32[4096]{0:T(1024)S(1)} %copy-done.14), kind=kOutput, calls=%fused_computation.25 | convolution fusion | flops 1388579712 | bytes 15436416 | tf_op jit(solution)/shard_map/tf,fd->td/dot_general | solution.py:256
  209.3 8.8 %collective-permute-done.8 = bf16[168,2048]{1,0:T(8,128)(2,1)S(1)} collective-permute-done((bf16[168,2048]{1,0:T(8,128)(2,1)S(1)}, bf16[168,2048]{1,0:T(8,128)(2,1)S(1)}, u32[]{:S(2)}, u32[]{:S(2)}) %collective-permute-start.8) | collective-permute-done | bytes 688160 | tf_op jit(solution)/shard_map/ppermute | solution.py:26
  218.2 1.8 multiply_convert_fusion
  219.9 0.5 collective-permute-start.10
  220.4 1.9 fusion.11
  222.3 9.7 %collective-permute-done.10 = bf16[168,2048]{1,0:T(8,128)(2,1)S(1)} collective-permute-done((bf16[168,2048]{1,0:T(8,128)(2,1)S(1)}, bf16[168,2048]{1,0:T(8,128)(2,1)S(1)}, u32[]{:S(2)}, u32[]{:S(2)}) %collective-permute-start.10) | collective-permute-done | bytes 688160 | tf_op jit(solution)/shard_map/ppermute | solution.py:36
  232.0 0.5 maximum_select_fusion
  232.5 1.1 fusion.29
  (26 shorter events, 0.1 us)
Async XLA Ops:
  0.6 3.3 %copy-start.3 = (f32[3,56,4096]{2,1,0:T(8,128)S(1)}, f32[3,56,4096]{2,1,0:T(8,128)}, u32[]{:S(2)}) copy-start(f32[3,56,4096]{2,1,0:T(8,128)} %param.11) | copy-start | bytes 8257540
  3.9 1.0 copy-start.11
  3.9 1.1 copy-start.12
  3.9 1.3 copy-start.13
  5.2 74.4 %copy-start.7 = (bf16[160,4096]{1,0:T(8,128)(2,1)S(1)}, bf16[160,4096]{1,0:T(8,128)(2,1)}, u32[]{:S(2)}) copy-start(bf16[160,4096]{1,0:T(8,128)(2,1)} %param.9) | copy-start | bytes 3932164
  76.2 3.4 %copy-start = (bf16[6,176,4096]{2,1,0:T(8,128)(2,1)}, bf16[6,176,4096]{2,1,0:T(8,128)(2,1)S(1)}, u32[]{:S(2)}) copy-start(bf16[6,176,4096]{2,1,0:T(8,128)(2,1)S(1)} %get-tuple-element.6) | copy-start | bytes 25952260
  83.7 4.5 %copy-start.2 = (bf16[160,4096]{1,0:T(8,128)(2,1)S(1)}, bf16[160,4096]{1,0:T(8,128)(2,1)}, u32[]{:S(2)}) copy-start(bf16[160,4096]{1,0:T(8,128)(2,1)} %param.8) | copy-start | bytes 3932164
  83.7 4.5 %copy-start.14 = (f32[4096]{0:T(1024)S(1)}, f32[4096]{0:T(1024)}, u32[]{:S(2)}) copy-start(f32[4096]{0:T(1024)} %param.12) | copy-start | bytes 49156
  88.6 6.4 %copy-start.8 = (bf16[160,4096]{1,0:T(8,128)(2,1)}, bf16[160,4096]{1,0:T(8,128)(2,1)S(1)}, u32[]{:S(2)}) copy-start(bf16[160,4096]{1,0:T(8,128)(2,1)S(1)} %fusion.7) | copy-start | bytes 3932164
  110.7 8.4 %copy-start.1 = (f32[1056,4096]{1,0:T(8,128)}, f32[1056,4096]{1,0:T(8,128)S(1)}, u32[]{:S(2)}) copy-start(f32[1056,4096]{1,0:T(8,128)S(1)} %fusion.13) | copy-start | bytes 51904516
  119.1 5.4 %collective-permute-start.3 = (f32[168,4096]{1,0:T(8,128)}, f32[168,4096]{1,0:T(8,128)}, u32[]{:S(2)}, u32[]{:S(2)}) collective-permute-start(f32[168,4096]{1,0:T(8,128)} %get-tuple-element.11), channel_id=1, source_target_pairs={{0,2},{2,0},{4,6},{6,4},{8,10},{10,8},{12,14},{14,12},{16,18},{18,... | collective-permute-start | bytes 8257544 | tf_op jit(solution)/shard_map/ppermute | solution.py:31
  119.4 9.0 %collective-permute-start.6 = (f32[168,4096]{1,0:T(8,128)}, f32[168,4096]{1,0:T(8,128)}, u32[]{:S(2)}, u32[]{:S(2)}) collective-permute-start(f32[168,4096]{1,0:T(8,128)} %get-tuple-element.12), channel_id=1, source_target_pairs={{0,2},{2,0},{4,6},{6,4},{8,10},{10,8},{12,14},{14,12},{16,18},{18,... | collective-permute-start | bytes 8257544 | tf_op jit(solution)/shard_map/ppermute | solution.py:31
  119.6 12.8 %collective-permute-start = (f32[168,4096]{1,0:T(8,128)}, f32[168,4096]{1,0:T(8,128)}, u32[]{:S(2)}, u32[]{:S(2)}) collective-permute-start(f32[168,4096]{1,0:T(8,128)} %get-tuple-element.13), channel_id=1, source_target_pairs={{0,2},{2,0},{4,6},{6,4},{8,10},{10,8},{12,14},{14,12},{16,18},{18,... | collective-permute-start | bytes 8257544 | tf_op jit(solution)/shard_map/ppermute | solution.py:31
  142.6 25.6 %copy-start.4 = (f32[168,4096]{1,0:T(8,128)}, f32[168,4096]{1,0:T(8,128)S(1)}, u32[]{:S(2)}) copy-start(f32[168,4096]{1,0:T(8,128)S(1)} %get-tuple-element.9) | copy-start | bytes 8257540
  142.6 20.9 %copy-start.6 = (f32[168,4096]{1,0:T(8,128)S(1)}, f32[168,4096]{1,0:T(8,128)}, u32[]{:S(2)}) copy-start(f32[168,4096]{1,0:T(8,128)} %get-tuple-element.8) | copy-start | bytes 8257540
  145.1 18.4 %collective-permute-start.1 = (bf16[168,2048]{1,0:T(8,128)(2,1)S(1)}, bf16[168,2048]{1,0:T(8,128)(2,1)S(1)}, u32[]{:S(2)}, u32[]{:S(2)}) collective-permute-start(bf16[168,2048]{1,0:T(8,128)(2,1)S(1)} %dynamic-slice_convert_fusion.3), channel_id=1, source_target_pairs={{0,1},{1,0},{2,3},{3,2},{4,5},{5,4},{6,7},{7,6},{8,9},{9,8},{10,11... | collective-permute-start | bytes 2064392 | tf_op jit(solution)/shard_map/ppermute | solution.py:36
  145.7 36.7 %copy-start.5 = (f32[168,4096]{1,0:T(8,128)S(1)}, f32[168,4096]{1,0:T(8,128)}, u32[]{:S(2)}) copy-start(f32[168,4096]{1,0:T(8,128)} %get-tuple-element.10) | copy-start | bytes 8257540
  147.3 31.0 %collective-permute-start.4 = (bf16[168,2048]{1,0:T(8,128)(2,1)S(1)}, bf16[168,2048]{1,0:T(8,128)(2,1)S(1)}, u32[]{:S(2)}, u32[]{:S(2)}) collective-permute-start(bf16[168,2048]{1,0:T(8,128)(2,1)S(1)} %dynamic-slice_convert_fusion.2), channel_id=1, source_target_pairs={{0,1},{1,0},{2,3},{3,2},{4,5},{5,4},{6,7},{7,6},{8,9},{9,8},{10,11... | collective-permute-start | bytes 2064392 | tf_op jit(solution)/shard_map/ppermute | solution.py:36
  163.7 18.7 %collective-permute-start.2 = (bf16[168,2048]{1,0:T(8,128)(2,1)S(1)}, bf16[168,2048]{1,0:T(8,128)(2,1)S(1)}, u32[]{:S(2)}, u32[]{:S(2)}) collective-permute-start(bf16[168,2048]{1,0:T(8,128)(2,1)S(1)} %add_convert_fusion.2), channel_id=1, source_target_pairs={{0,4},{2,6},{4,8},{6,10},{8,12},{10,14},{12,16},{14,18},{16,20},{1... | collective-permute-start | bytes 2064392 | tf_op jit(solution)/shard_map/ppermute | solution.py:26
  169.1 24.0 %collective-permute-start.7 = (bf16[168,2048]{1,0:T(8,128)(2,1)}, bf16[168,2048]{1,0:T(8,128)(2,1)}, u32[]{:S(2)}, u32[]{:S(2)}) collective-permute-start(bf16[168,2048]{1,0:T(8,128)(2,1)} %dynamic-slice_convert_fusion.1), channel_id=1, source_target_pairs={{0,1},{1,0},{2,3},{3,2},{4,5},{5,4},{6,7},{7,6},{8,9},{9,8},{10,11... | collective-permute-start | bytes 2064392 | tf_op jit(solution)/shard_map/ppermute | solution.py:36
  183.6 16.9 %collective-permute-start.5 = (bf16[168,2048]{1,0:T(8,128)(2,1)}, bf16[168,2048]{1,0:T(8,128)(2,1)}, u32[]{:S(2)}, u32[]{:S(2)}) collective-permute-start(bf16[168,2048]{1,0:T(8,128)(2,1)} %add_convert_fusion.1), channel_id=1, source_target_pairs={{0,4},{2,6},{4,8},{6,10},{8,12},{10,14},{12,16},{14,18},{16,20},{1... | collective-permute-start | bytes 2064392 | tf_op jit(solution)/shard_map/ppermute | solution.py:26
  183.9 19.5 %copy-start.9 = (bf16[160,6,56]{2,0,1:T(8,128)(2,1)S(1)}, bf16[160,6,56]{2,0,1:T(8,128)(2,1)}, u32[]{:S(2)}) copy-start(bf16[160,6,56]{2,0,1:T(8,128)(2,1)} %get-tuple-element.14) | copy-start | bytes 322564
  183.9 19.5 %copy-start.10 = (bf16[160,6,56]{2,0,1:T(8,128)(2,1)S(1)}, bf16[160,6,56]{2,0,1:T(8,128)(2,1)}, u32[]{:S(2)}) copy-start(bf16[160,6,56]{2,0,1:T(8,128)(2,1)} %get-tuple-element.15) | copy-start | bytes 322564
  183.9 19.5 %copy-start.15 = (f32[160,4096]{1,0:T(8,128)S(1)}, f32[160,4096]{1,0:T(8,128)}, u32[]{:S(2)}) copy-start(f32[160,4096]{1,0:T(8,128)} %param.10) | copy-start | bytes 7864324
  185.5 23.9 %collective-permute-start.9 = (bf16[168,2048]{1,0:T(8,128)(2,1)S(1)}, bf16[168,2048]{1,0:T(8,128)(2,1)S(1)}, u32[]{:S(2)}, u32[]{:S(2)}) collective-permute-start(bf16[168,2048]{1,0:T(8,128)(2,1)S(1)} %dynamic-slice_convert_fusion), channel_id=1, source_target_pairs={{2,3},{3,2},{6,7},{7,6},{10,11},{11,10},{14,15},{15,14},{18,19},{1... | collective-permute-start | bytes 2064392 | tf_op jit(solution)/shard_map/ppermute | solution.py:46
  202.5 15.7 %collective-permute-start.8 = (bf16[168,2048]{1,0:T(8,128)(2,1)S(1)}, bf16[168,2048]{1,0:T(8,128)(2,1)S(1)}, u32[]{:S(2)}, u32[]{:S(2)}) collective-permute-start(bf16[168,2048]{1,0:T(8,128)(2,1)S(1)} %add_convert_fusion), channel_id=1, source_target_pairs={{0,4},{2,6},{4,8},{6,10},{8,12},{10,14},{12,16},{14,18},{16,20},{1... | collective-permute-start | bytes 2064392 | tf_op jit(solution)/shard_map/ppermute | solution.py:26
  219.9 12.1 %collective-permute-start.10 = (bf16[168,2048]{1,0:T(8,128)(2,1)S(1)}, bf16[168,2048]{1,0:T(8,128)(2,1)S(1)}, u32[]{:S(2)}, u32[]{:S(2)}) collective-permute-start(bf16[168,2048]{1,0:T(8,128)(2,1)S(1)} %multiply_convert_fusion), channel_id=1, source_target_pairs={{0,1},{1,0},{2,3},{3,2},{4,5},{5,4},{6,7},{7,6},{8,9},{9,8},{10,11... | collective-permute-start | bytes 2064392 | tf_op jit(solution)/shard_map/ppermute | solution.py:36

commit v3 on v2

--- a/solution.py
+++ b/solution.py
@@ -240,19 +240,18 @@
     flat = groups.reshape(count * rows, width)
     left = jnp.einsum("td,fd->tf", normed, flat, preferred_element_type=jnp.float32)
     right = jnp.einsum("td,fd->tf", grad_in, flat, preferred_element_type=jnp.float32)
-    left = left.reshape(tokens, count, rows)
-    gate, upper = left[:, :, :units], left[:, :, units : 2 * units]
-    dhidden = right.reshape(tokens, count, rows)[:, :, 2 * units : 3 * units]
+    lane = lax.broadcasted_iota(jnp.int32, (1, count * rows), 1)
+    used = lax.rem(lane, rows) < units
+    gate, upper = left, jnp.roll(left, -units, axis=1)
+    dhidden = jnp.roll(right, -2 * units, axis=1)
     sigma = jax.nn.sigmoid(gate)
     act = gate * sigma
-    hidden = (act * upper).astype(jnp.bfloat16)
-    dgate = (dhidden * upper * sigma * (1.0 + gate * (1.0 - sigma))).astype(jnp.bfloat16)
-    dup = (dhidden * act).astype(jnp.bfloat16)
-    rest = rows - 2 * units
-    dgu = jnp.pad(jnp.concatenate([dgate, dup], axis=2), ((0, 0), (0, 0), (0, rest)))
-    dgu = dgu.reshape(tokens, count * rows)
-    hid = jnp.pad(hidden, ((0, 0), (0, 0), (2 * units, rest - units)))
-    hid = hid.reshape(tokens, count * rows)
+    hidden = jnp.where(used, act * upper, 0.0).astype(jnp.bfloat16)
+    dgate = dhidden * upper * sigma * (1.0 + gate * (1.0 - sigma))
+    dgate = jnp.where(used, dgate, 0.0).astype(jnp.bfloat16)
+    dup = jnp.where(used, dhidden * act, 0.0).astype(jnp.bfloat16)
+    dgu = dgate + jnp.roll(dup, units, axis=1)
+    hid = jnp.roll(hidden, 2 * units, axis=1)
     dnormed = jnp.einsum("tf,fd->td", dgu, flat, preferred_element_type=jnp.float32)
     terms = jnp.einsum(
         "tf,td->fd",

time: 234 us -> 214 us (0.915)
  local copies, waits for them, and re-layouts: 33.8 us -> 20.3 us
  matrix products: 22.6 us -> 17.2 us
    reshape x3 -> x0, local copies, waits for them, and re-layouts: 7.66 us -> none  [the longest x1 2.98 us: group_terms(): dhidden = right.reshape(tokens, count, rows)[:, :, 2 * units:3 * units]]
    dot_general x1, matrix products: 6.33 us -> 3.22 us  [group_terms(): jnp.einsum('td,fd->tf', normed, flat, preferred_element_type=jnp.float32)]
    unnamed x33 -> x30, local copies, waits for them, and re-layouts: 9.14 us -> 6.51 us
where the time goes in v3:
time: 214 us; the launch traced here: 213 us
  waiting for transfers between devices  72.6 us (34%)
  Pallas kernels  70.6 us (33%)
  other arithmetic  21.2 us (10%)
  local copies, waits for them, and re-layouts  20.3 us (9%)
  matrix products  17.2 us (8%)
  starting transfers between devices  10.6 us (5%)
    pallas_call x1, Pallas kernels, gathered(): pl.pallas_call(lambda *refs: gather_kernel(chips, *refs), out_shape=(jax....  70.6 us
    ppermute x4, waiting for transfers between devices, swapped_rep(): lax.ppermute(value, 'rep', [(i, (i + 1) % count) for i in range(count)])  39.9 us
    ppermute x3, waiting for transfers between devices, moved(): lax.ppermute(value, 'blk', [(i, (i + steps) % count) for i in range(count)])  20.3 us
    ppermute x3, waiting for transfers between devices, swapped_core(): return lax.ppermute(value, 'blk', [(i, i ^ 1) for i in range(count)])  12.4 us
    add x1, other arithmetic, shards(): last = own_term + jnp.where(core == 0, received, 0.0)  10.4 us
    unnamed x30, local copies, waits for them, and re-layouts  6.51 us
    dot_general x1, matrix products, group_terms(): jnp.einsum('tf,fd->td', dgu, flat, preferred_element_type=jnp.float32)  5.83 us
    ppermute x3, starting transfers between devices, moved(): lax.ppermute(value, 'blk', [(i, (i + steps) % count) for i in range(count)])  5.73 us
  transfers between devices with their start and end apart: 11, of which 10 were waited for; matrix products, arithmetic and copies ran while one was open for 7% of the time, Pallas kernels for 0%

profile of v3, /device:TPU:0, one launch (start us, length us, event | category | flops | bytes accessed | tf_op | source)
XLA Modules:
  0.0 213.4 jit_solution(13073271166658442336)
XLA Ops:
  0.7 1.7 fusion.4
  2.3 1.6 fusion.16.refs_2_
  3.9 0.6 copy-done.3
  4.5 0.0 copy-start.13
  4.5 0.1 pad_dynamic-slice_fusion.1.refs_1_
  4.7 0.1 pad.24.clone
  4.7 1.1 copy-done.2
  5.8 0.0 copy-done.14
  5.8 0.4 fusion.6
  6.2 0.0 copy-done.11
  6.3 0.0 copy-done.12
  6.3 0.0 copy-done.13
  6.3 0.3 maximum_maximum_fusion.refs_0_
  6.6 70.6 %gather_weights.1 = (bf16[6,176,4096]{2,1,0:T(8,128)(2,1)S(1)}, bf16[176,2048]{1,0:T(8,128)(2,1)S(1)}) custom-call(bf16[176,4096]{1,0:T(8,128)(2,1)S(1)} %maximum_maximum_fusion.refs_0_, f32[176,2048]{1,0:T(8,128)S(1)} %pad_dynamic-slice_fusion.1.refs_1_, bf16[176,2048]{1,0:T(8,128)(2,1)S(1)} %fusion.16.refs_2_), custom_call_target="tpu_custom_call" | custom-call | tf_op jit(solution)/shard_map/gather_weights/pallas_call | solution.py:206
  77.2 0.0 copy-start
  77.2 0.0 copy-start.7
  77.2 3.2 %fusion.24 = f32[160,1056]{1,0:T(8,128)S(1)} fusion(bf16[160,4096]{1,0:T(8,128)(2,1)S(1)} %fusion.6, bf16[1056,4096]{1,0:T(8,128)(2,1)S(1)} %bitcast.29), kind=kOutput, calls=%fused_computation.59 | convolution fusion | flops 1384120320 | bytes 10637312 | tf_op jit(solution)/shard_map/td,fd->tf/dot_general | solution.py:241
  80.5 0.2 slice.89
  80.7 3.2 %convolution_bitcast_fusion = f32[160,1056]{1,0:T(8,128)S(1)} fusion(bf16[1056,4096]{1,0:T(8,128)(2,1)S(1)} %bitcast.30, bf16[160,4096]{1,0:T(8,128)(2,1)S(1)} %copy-done.7), kind=kOutput, calls=%fused_computation.29 | convolution fusion | flops 1384120320 | bytes 10637312 | tf_op jit(solution)/shard_map/td,fd->tf/dot_general | solution.py:242
  84.0 0.2 slice.87
  84.2 0.3 select_convert_fusion
  84.6 0.1 slice.93
  84.7 0.1 slice.91
  84.8 0.5 maximum_add_fusion
  85.3 0.0 copy-start.8
  85.3 5.0 %fusion.12 = f32[1056,4096]{1,0:T(8,128)S(1)} fusion(bf16[160,4096]{1,0:T(8,128)(2,1)S(1)} %copy-done.7, bf16[160,4096]{1,0:T(8,128)(2,1)S(1)} %fusion.6, bf16[160,944]{1,0:T(8,128)(2,1)S(1)} %slice.94, bf16[160,112]{1,0:T(8,128)(2,1)S(1)} %slice.93, bf16[160,1056]{1,0:T(8,128)(2,1)S(1)} %maximum_add_fusion), kind=kOutput, calls=%fused_computation.25 | convolution fusion | flops 2775511040 | bytes 20598784 | tf_op jit(solution)/shard_map/tf,td->fd/dot_general | solution.py:256
  90.3 3.7 %slice_bitcast_fusion.2 = (f32[168,4096]{1,0:T(8,128)}, f32[168,4096]{1,0:T(8,128)}, f32[168,4096]{1,0:T(8,128)}) fusion(f32[6,176,4096]{2,1,0:T(8,128)S(1)} %bitcast.32), kind=kLoop, calls=%fused_computation.11 | loop fusion | bytes 16515072 | tf_op jit(solution)/shard_map/squeeze | solution.py:303
  94.0 4.8 %copy-done.1 = f32[1056,4096]{1,0:T(8,128)} copy-done((f32[1056,4096]{1,0:T(8,128)}, f32[1056,4096]{1,0:T(8,128)S(1)}, u32[]{:S(2)}) %copy-start.1) | copy-done | bytes 17301528
  98.7 0.4 collective-permute-start.3
  99.1 0.1 collective-permute-start.6
  99.2 0.4 collective-permute-start
  99.6 4.6 %collective-permute-done.3 = f32[168,4096]{1,0:T(8,128)} collective-permute-done((f32[168,4096]{1,0:T(8,128)}, f32[168,4096]{1,0:T(8,128)}, u32[]{:S(2)}, u32[]{:S(2)}) %collective-permute-start.3) | collective-permute-done | bytes 2752544 | tf_op jit(solution)/shard_map/ppermute | solution.py:31
  104.2 3.9 %collective-permute-done.6 = f32[168,4096]{1,0:T(8,128)} collective-permute-done((f32[168,4096]{1,0:T(8,128)}, f32[168,4096]{1,0:T(8,128)}, u32[]{:S(2)}, u32[]{:S(2)}) %collective-permute-start.6) | collective-permute-done | bytes 2752544 | tf_op jit(solution)/shard_map/ppermute | solution.py:31
  108.1 3.9 %collective-permute-done = f32[168,4096]{1,0:T(8,128)} collective-permute-done((f32[168,4096]{1,0:T(8,128)}, f32[168,4096]{1,0:T(8,128)}, u32[]{:S(2)}, u32[]{:S(2)}) %collective-permute-start) | collective-permute-done | bytes 2752544 | tf_op jit(solution)/shard_map/ppermute | solution.py:31
  112.0 10.4 %fusion.3 = (f32[168,4096]{1,0:T(8,128)}, f32[168,4096]{1,0:T(8,128)S(1)}, f32[168,4096]{1,0:T(8,128)}) fusion(f32[6,176,4096]{2,1,0:T(8,128)} %bitcast.33, f32[168,4096]{1,0:T(8,128)} %collective-permute-done, pred[]{:T(512)S(6)} %eq.8, f32[168,4096]{1,0:T(8,128)} %collective-permute-done.6, f32[168,4096]{1,0:T(8,128)} %collective-permute-done.3), kind=kLoop, calls=%fused_computation.16 | loop fusion | flops 2752512 | bytes 24772608 | tf_op jit(solution)/shard_map/add | solution.py:308
  122.5 2.5 %dynamic-slice_convert_fusion.3 = bf16[168,2048]{1,0:T(8,128)(2,1)S(1)} fusion(f32[168,4096]{1,0:T(8,128)} %get-tuple-element.8, s32[]{:T(128)S(6)} %select_n.49), kind=kLoop, calls=%fused_computation.40 | loop fusion | bytes 1376260 | tf_op jit(solution)/shard_map/convert_element_type | solution.py:283
  124.9 0.6 collective-permute-start.1
  125.5 1.6 dynamic-slice_convert_fusion.2
  127.1 1.6 collective-permute-start.4
  128.7 14.7 %collective-permute-done.1 = bf16[168,2048]{1,0:T(8,128)(2,1)S(1)} collective-permute-done((bf16[168,2048]{1,0:T(8,128)(2,1)S(1)}, bf16[168,2048]{1,0:T(8,128)(2,1)S(1)}, u32[]{:S(2)}, u32[]{:S(2)}) %collective-permute-start.1) | collective-permute-done | bytes 688160 | tf_op jit(solution)/shard_map/ppermute | solution.py:36
  143.4 0.2 add_convert_fusion.2
  143.5 4.5 %collective-permute-start.2 = (bf16[168,2048]{1,0:T(8,128)(2,1)S(1)}, bf16[168,2048]{1,0:T(8,128)(2,1)S(1)}, u32[]{:S(2)}, u32[]{:S(2)}) collective-permute-start(bf16[168,2048]{1,0:T(8,128)(2,1)S(1)} %add_convert_fusion.2), channel_id=1, source_target_pairs={{0,4},{2,6},{4,8},{6,10},{8,12},{10,14},{12,16},{14,18},{16,20},{1... | collective-permute-start | bytes 2064392 | tf_op jit(solution)/shard_map/ppermute | solution.py:26
  148.0 0.0 copy-done.4
  148.0 0.9 dynamic-slice_convert_fusion.1
  148.9 0.6 collective-permute-start.7
  149.5 8.6 %collective-permute-done.4 = bf16[168,2048]{1,0:T(8,128)(2,1)S(1)} collective-permute-done((bf16[168,2048]{1,0:T(8,128)(2,1)S(1)}, bf16[168,2048]{1,0:T(8,128)(2,1)S(1)}, u32[]{:S(2)}, u32[]{:S(2)}) %collective-permute-start.4) | collective-permute-done | bytes 688160 | tf_op jit(solution)/shard_map/ppermute | solution.py:36
  158.1 4.1 %collective-permute-done.2 = bf16[168,2048]{1,0:T(8,128)(2,1)S(1)} collective-permute-done((bf16[168,2048]{1,0:T(8,128)(2,1)S(1)}, bf16[168,2048]{1,0:T(8,128)(2,1)S(1)}, u32[]{:S(2)}, u32[]{:S(2)}) %collective-permute-start.2) | collective-permute-done | bytes 688160 | tf_op jit(solution)/shard_map/ppermute | solution.py:26
  162.2 1.2 add_convert_fusion.1
  163.4 0.3 collective-permute-start.5
  163.7 1.6 dynamic-slice_convert_fusion
  165.3 0.7 collective-permute-start.9
  166.0 7.0 %collective-permute-done.7 = bf16[168,2048]{1,0:T(8,128)(2,1)} collective-permute-done((bf16[168,2048]{1,0:T(8,128)(2,1)}, bf16[168,2048]{1,0:T(8,128)(2,1)}, u32[]{:S(2)}, u32[]{:S(2)}) %collective-permute-start.7) | collective-permute-done | bytes 688160 | tf_op jit(solution)/shard_map/ppermute | solution.py:36
  173.0 7.3 %collective-permute-done.5 = bf16[168,2048]{1,0:T(8,128)(2,1)} collective-permute-done((bf16[168,2048]{1,0:T(8,128)(2,1)}, bf16[168,2048]{1,0:T(8,128)(2,1)}, u32[]{:S(2)}, u32[]{:S(2)}) %collective-permute-start.5) | collective-permute-done | bytes 688160 | tf_op jit(solution)/shard_map/ppermute | solution.py:26
  180.3 2.0 add_convert_fusion
  182.3 0.9 collective-permute-start.8
  183.2 5.8 %fusion.11 = (f32[160]{0:T(256)S(1)}, f32[160,4096]{1,0:T(8,128)S(1)}) fusion(bf16[160,4096]{1,0:T(8,128)(2,1)S(1)} %copy-done.2, f32[160,4096]{1,0:T(8,128)S(1)} %copy-done.10, bf16[160,1056]{1,0:T(8,128)(2,1)S(1)} %copy-done.9, bf16[1056,4096]{1,0:T(8,128)(2,1)} %bitcast.31, f32[4096]{0:T(1024)S(1)} %copy-done.14), kind=kOutput, calls=%fused_computation.24 | convolution fusion | flops 1387396992 | bytes 15559296 | tf_op jit(solution)/shard_map/tf,fd->td/dot_general | solution.py:255
  189.0 0.0 collective-permute-done.9
  189.0 8.9 %collective-permute-done.8 = bf16[168,2048]{1,0:T(8,128)(2,1)S(1)} collective-permute-done((bf16[168,2048]{1,0:T(8,128)(2,1)S(1)}, bf16[168,2048]{1,0:T(8,128)(2,1)S(1)}, u32[]{:S(2)}, u32[]{:S(2)}) %collective-permute-start.8) | collective-permute-done | bytes 688160 | tf_op jit(solution)/shard_map/ppermute | solution.py:26
  197.9 1.8 multiply_convert_fusion
  199.7 0.5 collective-permute-start.10
  200.2 1.9 fusion.10
  202.2 9.6 %collective-permute-done.10 = bf16[168,2048]{1,0:T(8,128)(2,1)S(1)} collective-permute-done((bf16[168,2048]{1,0:T(8,128)(2,1)S(1)}, bf16[168,2048]{1,0:T(8,128)(2,1)S(1)}, u32[]{:S(2)}, u32[]{:S(2)}) %collective-permute-start.10) | collective-permute-done | bytes 688160 | tf_op jit(solution)/shard_map/ppermute | solution.py:36
  211.8 0.5 maximum_select_fusion
  212.3 1.1 fusion.23
  (26 shorter events, 0.1 us)
Async XLA Ops:
  2.3 2.2 %copy-start.3 = (f32[3,56,4096]{2,1,0:T(8,128)S(1)}, f32[3,56,4096]{2,1,0:T(8,128)}, u32[]{:S(2)}) copy-start(f32[3,56,4096]{2,1,0:T(8,128)} %param.11) | copy-start | bytes 8257540
  4.5 1.3 copy-start.2
  4.5 1.3 copy-start.14
  4.5 1.7 copy-start.11
  4.5 1.7 copy-start.12
  4.5 1.7 copy-start.13
  77.2 3.5 %copy-start = (bf16[6,176,4096]{2,1,0:T(8,128)(2,1)}, bf16[6,176,4096]{2,1,0:T(8,128)(2,1)S(1)}, u32[]{:S(2)}) copy-start(bf16[6,176,4096]{2,1,0:T(8,128)(2,1)S(1)} %get-tuple-element.6) | copy-start | bytes 25952260
  77.2 3.5 %copy-start.7 = (bf16[160,4096]{1,0:T(8,128)(2,1)S(1)}, bf16[160,4096]{1,0:T(8,128)(2,1)}, u32[]{:S(2)}) copy-start(bf16[160,4096]{1,0:T(8,128)(2,1)} %param.9) | copy-start | bytes 3932164
  85.3 5.0 %copy-start.8 = (bf16[160,1056]{1,0:T(8,128)(2,1)}, bf16[160,1056]{1,0:T(8,128)(2,1)S(1)}, u32[]{:S(2)}) copy-start(bf16[160,1056]{1,0:T(8,128)(2,1)S(1)} %maximum_add_fusion) | copy-start | bytes 1013764
  90.3 8.4 %copy-start.1 = (f32[1056,4096]{1,0:T(8,128)}, f32[1056,4096]{1,0:T(8,128)S(1)}, u32[]{:S(2)}) copy-start(f32[1056,4096]{1,0:T(8,128)S(1)} %fusion.12) | copy-start | bytes 51904516
  98.7 5.4 %collective-permute-start.3 = (f32[168,4096]{1,0:T(8,128)}, f32[168,4096]{1,0:T(8,128)}, u32[]{:S(2)}, u32[]{:S(2)}) collective-permute-start(f32[168,4096]{1,0:T(8,128)} %get-tuple-element.11), channel_id=1, source_target_pairs={{0,2},{2,0},{4,6},{6,4},{8,10},{10,8},{12,14},{14,12},{16,18},{18,... | collective-permute-start | bytes 8257544 | tf_op jit(solution)/shard_map/ppermute | solution.py:31
  99.1 9.0 %collective-permute-start.6 = (f32[168,4096]{1,0:T(8,128)}, f32[168,4096]{1,0:T(8,128)}, u32[]{:S(2)}, u32[]{:S(2)}) collective-permute-start(f32[168,4096]{1,0:T(8,128)} %get-tuple-element.12), channel_id=1, source_target_pairs={{0,2},{2,0},{4,6},{6,4},{8,10},{10,8},{12,14},{14,12},{16,18},{18,... | collective-permute-start | bytes 8257544 | tf_op jit(solution)/shard_map/ppermute | solution.py:31
  99.2 12.8 %collective-permute-start = (f32[168,4096]{1,0:T(8,128)}, f32[168,4096]{1,0:T(8,128)}, u32[]{:S(2)}, u32[]{:S(2)}) collective-permute-start(f32[168,4096]{1,0:T(8,128)} %get-tuple-element.13), channel_id=1, source_target_pairs={{0,2},{2,0},{4,6},{6,4},{8,10},{10,8},{12,14},{14,12},{16,18},{18,... | collective-permute-start | bytes 8257544 | tf_op jit(solution)/shard_map/ppermute | solution.py:31
  122.5 25.5 %copy-start.4 = (f32[168,4096]{1,0:T(8,128)}, f32[168,4096]{1,0:T(8,128)S(1)}, u32[]{:S(2)}) copy-start(f32[168,4096]{1,0:T(8,128)S(1)} %get-tuple-element.9) | copy-start | bytes 8257540
  122.5 20.9 %copy-start.6 = (f32[168,4096]{1,0:T(8,128)S(1)}, f32[168,4096]{1,0:T(8,128)}, u32[]{:S(2)}) copy-start(f32[168,4096]{1,0:T(8,128)} %get-tuple-element.8) | copy-start | bytes 8257540
  124.9 18.4 %collective-permute-start.1 = (bf16[168,2048]{1,0:T(8,128)(2,1)S(1)}, bf16[168,2048]{1,0:T(8,128)(2,1)S(1)}, u32[]{:S(2)}, u32[]{:S(2)}) collective-permute-start(bf16[168,2048]{1,0:T(8,128)(2,1)S(1)} %dynamic-slice_convert_fusion.3), channel_id=1, source_target_pairs={{0,1},{1,0},{2,3},{3,2},{4,5},{5,4},{6,7},{7,6},{8,9},{9,8},{10,11... | collective-permute-start | bytes 2064392 | tf_op jit(solution)/shard_map/ppermute | solution.py:36
  125.5 36.7 %copy-start.5 = (f32[168,4096]{1,0:T(8,128)S(1)}, f32[168,4096]{1,0:T(8,128)}, u32[]{:S(2)}) copy-start(f32[168,4096]{1,0:T(8,128)} %get-tuple-element.10) | copy-start | bytes 8257540
  127.1 31.0 %collective-permute-start.4 = (bf16[168,2048]{1,0:T(8,128)(2,1)S(1)}, bf16[168,2048]{1,0:T(8,128)(2,1)S(1)}, u32[]{:S(2)}, u32[]{:S(2)}) collective-permute-start(bf16[168,2048]{1,0:T(8,128)(2,1)S(1)} %dynamic-slice_convert_fusion.2), channel_id=1, source_target_pairs={{0,1},{1,0},{2,3},{3,2},{4,5},{5,4},{6,7},{7,6},{8,9},{9,8},{10,11... | collective-permute-start | bytes 2064392 | tf_op jit(solution)/shard_map/ppermute | solution.py:36
  143.5 18.7 %collective-permute-start.2 = (bf16[168,2048]{1,0:T(8,128)(2,1)S(1)}, bf16[168,2048]{1,0:T(8,128)(2,1)S(1)}, u32[]{:S(2)}, u32[]{:S(2)}) collective-permute-start(bf16[168,2048]{1,0:T(8,128)(2,1)S(1)} %add_convert_fusion.2), channel_id=1, source_target_pairs={{0,4},{2,6},{4,8},{6,10},{8,12},{10,14},{12,16},{14,18},{16,20},{1... | collective-permute-start | bytes 2064392 | tf_op jit(solution)/shard_map/ppermute | solution.py:26
  148.9 24.0 %collective-permute-start.7 = (bf16[168,2048]{1,0:T(8,128)(2,1)}, bf16[168,2048]{1,0:T(8,128)(2,1)}, u32[]{:S(2)}, u32[]{:S(2)}) collective-permute-start(bf16[168,2048]{1,0:T(8,128)(2,1)} %dynamic-slice_convert_fusion.1), channel_id=1, source_target_pairs={{0,1},{1,0},{2,3},{3,2},{4,5},{5,4},{6,7},{7,6},{8,9},{9,8},{10,11... | collective-permute-start | bytes 2064392 | tf_op jit(solution)/shard_map/ppermute | solution.py:36
  163.4 16.9 %collective-permute-start.5 = (bf16[168,2048]{1,0:T(8,128)(2,1)}, bf16[168,2048]{1,0:T(8,128)(2,1)}, u32[]{:S(2)}, u32[]{:S(2)}) collective-permute-start(bf16[168,2048]{1,0:T(8,128)(2,1)} %add_convert_fusion.1), channel_id=1, source_target_pairs={{0,4},{2,6},{4,8},{6,10},{8,12},{10,14},{12,16},{14,18},{16,20},{1... | collective-permute-start | bytes 2064392 | tf_op jit(solution)/shard_map/ppermute | solution.py:26
  163.7 19.5 %copy-start.9 = (bf16[160,1056]{1,0:T(8,128)(2,1)S(1)}, bf16[160,1056]{1,0:T(8,128)(2,1)}, u32[]{:S(2)}) copy-start(bf16[160,1056]{1,0:T(8,128)(2,1)} %copy-done.8) | copy-start | bytes 1013764
  163.7 19.5 %copy-start.10 = (f32[160,4096]{1,0:T(8,128)S(1)}, f32[160,4096]{1,0:T(8,128)}, u32[]{:S(2)}) copy-start(f32[160,4096]{1,0:T(8,128)} %param.10) | copy-start | bytes 7864324
  165.3 23.7 %collective-permute-start.9 = (bf16[168,2048]{1,0:T(8,128)(2,1)S(1)}, bf16[168,2048]{1,0:T(8,128)(2,1)S(1)}, u32[]{:S(2)}, u32[]{:S(2)}) collective-permute-start(bf16[168,2048]{1,0:T(8,128)(2,1)S(1)} %dynamic-slice_convert_fusion), channel_id=1, source_target_pairs={{2,3},{3,2},{6,7},{7,6},{10,11},{11,10},{14,15},{15,14},{18,19},{1... | collective-permute-start | bytes 2064392 | tf_op jit(solution)/shard_map/ppermute | solution.py:46
  182.3 15.7 %collective-permute-start.8 = (bf16[168,2048]{1,0:T(8,128)(2,1)S(1)}, bf16[168,2048]{1,0:T(8,128)(2,1)S(1)}, u32[]{:S(2)}, u32[]{:S(2)}) collective-permute-start(bf16[168,2048]{1,0:T(8,128)(2,1)S(1)} %add_convert_fusion), channel_id=1, source_target_pairs={{0,4},{2,6},{4,8},{6,10},{8,12},{10,14},{12,16},{14,18},{16,20},{1... | collective-permute-start | bytes 2064392 | tf_op jit(solution)/shard_map/ppermute | solution.py:26
  199.7 12.1 %collective-permute-start.10 = (bf16[168,2048]{1,0:T(8,128)(2,1)S(1)}, bf16[168,2048]{1,0:T(8,128)(2,1)S(1)}, u32[]{:S(2)}, u32[]{:S(2)}) collective-permute-start(bf16[168,2048]{1,0:T(8,128)(2,1)S(1)} %multiply_convert_fusion), channel_id=1, source_target_pairs={{0,1},{1,0},{2,3},{3,2},{4,5},{5,4},{6,7},{7,6},{8,9},{9,8},{10,11... | collective-permute-start | bytes 2064392 | tf_op jit(solution)/shard_map/ppermute | solution.py:36
